TPU v7x, 32 devices: a whole 2x2x4 slice. The times are simulated.
32 devices in a mesh: rows: 2 (over core), ha: 4 (over y, x), ma: 4 (over z).
Axes of the slice: x: 2, y: 2, z: 4, core: 2. Of those that a mesh axis runs over, the one named last changes fastest.
Arguments:
- tokens: bfloat16 [32768, 1024], P(('rows', 'ha', 'ma')), may hold values from -6 to 6
- first_values: bfloat16 [32768, 1024], P(('rows', 'ha', 'ma')), may hold values from -6 to 6
- lengths: int32 [32], P(('rows', 'ha', 'ma')), may hold values from 128 to 1024, as said below
- w_query: bfloat16 [1024, 1024], replicated, may hold values from -0.25 to 0.25
- w_key: bfloat16 [1024, 1024], replicated, may hold values from -0.25 to 0.25
- w_value: bfloat16 [1024, 1024], replicated, may hold values from -0.1875 to 0.1875
- w_out: bfloat16 [1024, 1024], replicated, may hold values from -3 to 3
- norm_attn: float32 [1024], replicated, may hold values from 0.5 to 1.5
- norm_mlp: float32 [1024], replicated, may hold values from 0.5 to 1.5
- w_gate: bfloat16 [1024, 2816], P('ma', 'ha'), may hold values from -0.1875 to 0.1875
- w_up: bfloat16 [1024, 2816], P('ma', 'ha'), may hold values from -0.1875 to 0.1875
- w_down: bfloat16 [2816, 1024], P('ha', 'ma'), may hold values from -0.21875 to 0.21875
- grad_out: bfloat16 [32768, 1024], P(('rows', 'ha', 'ma')), may hold values from -6 to 6
Outputs:
- mixed_out: bfloat16 [32768, 1024], P(('rows', 'ha', 'ma'))
- grad_tokens: float32 [32768, 1024], P(('rows', 'ha', 'ma'))
- grad_first: float32 [32768, 1024], P(('rows', 'ha', 'ma'))
- grad_query: float32 [1024, 1024], replicated
- grad_key: float32 [1024, 1024], replicated
- grad_value: float32 [1024, 1024], replicated
- grad_wout: float32 [1024, 1024], replicated
- grad_norm_attn: float32 [1024], replicated
- grad_norm_mlp: float32 [1024], replicated
- grad_gate: float32 [1024, 2816], P('ma', 'ha')
- grad_up: float32 [1024, 2816], P('ma', 'ha')
- grad_down: float32 [2816, 1024], P('ha', 'ma')
Inputs may be any that keep to these rules, and one draw needn't show every extreme that they name: `lengths`: at least one sequence has exactly 1024 valid tokens in every draw.
All inputs are finite; a program needn't handle non-finite values.
Results may differ from a plain program's by a relative error of at most 0.017.
Values may be sent and summed in bfloat16 or wider, within the bound.
A program may use at most 320 MiB of HBM per device.

v0:
```python
import math

import jax
import jax.numpy as jnp
from jax import lax
from jax.sharding import PartitionSpec as P

D = 1024
H = 16
HD = 64
SLOT = 1024
QBLOCK = 512


def norm_rows(values, scales):
    return values * lax.rsqrt(jnp.mean(values * values, axis=-1, keepdims=True) + 1e-06) * scales


def rotate(values):
    halfway = values.shape[-1] // 2
    places = jnp.arange(values.shape[1], dtype=jnp.float32)
    frequency = 10000.0 ** (-jnp.arange(halfway, dtype=jnp.float32) * 2.0 / values.shape[-1])
    angles = places[:, None] * frequency[None, :]
    cosine = jnp.cos(angles)[None, :, None, :]
    sine_part = jnp.sin(angles)[None, :, None, :]
    first_half = values[..., :halfway]
    second_half = values[..., halfway:]
    return jnp.concatenate(
        [
            first_half * cosine - second_half * sine_part,
            second_half * cosine + first_half * sine_part,
        ],
        axis=-1,
    )


def unrotate(grads):
    unused, pullback = jax.vjp(rotate, grads)
    return pullback(grads)[0]


def contract(left, right, left_dim, right_dim):
    return lax.dot_general(
        left, right, (((left_dim,), (right_dim,)), ((), ())), preferred_element_type=jnp.float32
    )


def visible_mask(block_num, top, length):
    query_pos = block_num * QBLOCK + jnp.arange(QBLOCK, dtype=jnp.int32)
    key_pos = jnp.arange(top, dtype=jnp.int32)
    return (key_pos[None, :] <= query_pos[:, None]) & (key_pos[None, :] < length)


def block_scores(queries, keys_rot, block_num, top, length):
    scaling = 1.0 / math.sqrt(HD)
    block_q = queries[block_num * QBLOCK : top]
    scores = (
        jnp.einsum("qhd,khd->hqk", block_q, keys_rot[:top], preferred_element_type=jnp.float32)
        * scaling
    )
    return (jnp.where(visible_mask(block_num, top, length)[None], scores, -1e30), block_q)


def attend_forward(element):
    queries, keys_rot, values_mix, length = element
    outputs = []
    log_totals = []
    for block_num in range(SLOT // QBLOCK):
        top = (block_num + 1) * QBLOCK
        scores, block_q = block_scores(queries, keys_rot, block_num, top, length)
        maximum = jnp.max(scores, axis=-1, keepdims=True)
        exponent = jnp.exp(scores - maximum)
        denominator = jnp.sum(exponent, axis=-1, keepdims=True)
        probabilities = (exponent / denominator).astype(jnp.bfloat16)
        result = jnp.einsum(
            "hqk,khd->qhd", probabilities, values_mix[:top], preferred_element_type=jnp.float32
        )
        outputs.append(result.astype(jnp.bfloat16))
        log_totals.append(maximum[..., 0] + jnp.log(denominator[..., 0]))
    return (jnp.concatenate(outputs, axis=0), jnp.concatenate(log_totals, axis=1))


def attend_backward(element):
    queries, keys_rot, values_mix, grad_heads, log_totals, length = element
    scaling = 1.0 / math.sqrt(HD)
    grad_query_parts = []
    grad_keys = jnp.zeros(keys_rot.shape, jnp.float32)
    grad_values = jnp.zeros(values_mix.shape, jnp.float32)
    for block_num in range(SLOT // QBLOCK):
        top = (block_num + 1) * QBLOCK
        scores, block_q = block_scores(queries, keys_rot, block_num, top, length)
        probabilities = jnp.exp(scores - log_totals[:, block_num * QBLOCK : top, None])
        prob_low = probabilities.astype(jnp.bfloat16)
        block_grad = grad_heads[block_num * QBLOCK : top]
        grad_probs = jnp.einsum(
            "qhd,khd->hqk", block_grad, values_mix[:top], preferred_element_type=jnp.float32
        )
        grad_scores = probabilities * (
            grad_probs - jnp.sum(probabilities * grad_probs, axis=-1, keepdims=True)
        )
        score_low = grad_scores.astype(jnp.bfloat16)
        grad_query_parts.append(
            jnp.einsum(
                "hqk,khd->qhd", score_low, keys_rot[:top], preferred_element_type=jnp.float32
            )
            * scaling
        )
        grad_keys = grad_keys.at[:top].add(
            jnp.einsum("hqk,qhd->khd", score_low, block_q, preferred_element_type=jnp.float32)
            * scaling
        )
        grad_values = grad_values.at[:top].add(
            jnp.einsum("hqk,qhd->khd", prob_low, block_grad, preferred_element_type=jnp.float32)
        )
    return (jnp.concatenate(grad_query_parts, axis=0), grad_keys, grad_values)


def gate_grads(grad_hidden, gate, upper):
    sigma = jax.nn.sigmoid(gate)
    grad_upper = grad_hidden * gate * sigma
    grad_gate = grad_hidden * upper * sigma * (1.0 + gate * (1.0 - sigma))
    return (grad_gate.astype(jnp.bfloat16), grad_upper.astype(jnp.bfloat16))


def body(
    tokens,
    first_values,
    lengths,
    w_query,
    w_key,
    w_value,
    w_out,
    norm_attn,
    norm_mlp,
    w_gate,
    w_up,
    w_down,
    grad_out,
):
    tok_rows = tokens.shape[0]
    seq_count = lengths.shape[0]
    inputs = tokens.astype(jnp.float32)
    normed_a = norm_rows(inputs, norm_attn).astype(jnp.bfloat16)
    q_lin = jnp.dot(normed_a, w_query, preferred_element_type=jnp.float32)
    k_lin = jnp.dot(normed_a, w_key, preferred_element_type=jnp.float32)
    v_lin = jnp.dot(normed_a, w_value, preferred_element_type=jnp.float32)
    v_mix = (0.5 * v_lin + 0.5 * first_values.astype(jnp.float32)).astype(jnp.bfloat16)
    shape_four = (seq_count, SLOT, H, HD)
    q_rot = rotate(q_lin.reshape(shape_four)).astype(jnp.bfloat16)
    k_rot = rotate(k_lin.reshape(shape_four)).astype(jnp.bfloat16)
    v_heads = v_mix.reshape(shape_four)
    attended, log_totals = lax.map(attend_forward, (q_rot, k_rot, v_heads, lengths))
    attn_o = attended.reshape(tok_rows, D)
    h_one = inputs + jnp.dot(attn_o, w_out, preferred_element_type=jnp.float32)
    normed_m = norm_rows(h_one, norm_mlp).astype(jnp.bfloat16)
    gate_all, upper_all, down_all = (
        lax.all_gather(w_gate, "ma", axis=0, tiled=True),
        lax.all_gather(w_up, "ma", axis=0, tiled=True),
        lax.all_gather(w_down, "ma", axis=1, tiled=True),
    )
    features = lax.all_gather(normed_m, "ha", axis=0, tiled=True)
    gate = jnp.dot(features, gate_all, preferred_element_type=jnp.float32)
    upper = jnp.dot(features, upper_all, preferred_element_type=jnp.float32)
    hidden = (jax.nn.silu(gate) * upper).astype(jnp.bfloat16)
    branch = lax.psum_scatter(
        jnp.dot(
            lax.slice_in_dim(hidden, 0, lax.axis_size("ha") * tok_rows, axis=0),
            down_all,
            preferred_element_type=jnp.float32,
        ).astype(jnp.bfloat16),
        "ha",
        scatter_dimension=0,
        tiled=True,
    ).astype(jnp.float32)
    cotangent = lax.all_gather(grad_out, "ha", axis=0, tiled=True)
    grad_hidden = contract(cotangent, down_all, 1, 1)
    grad_gate, grad_upper = gate_grads(grad_hidden, gate, upper)
    gate_rows = lax.slice_in_dim(grad_gate, 0, lax.axis_size("ha") * tok_rows, axis=0)
    upper_rows = lax.slice_in_dim(grad_upper, 0, lax.axis_size("ha") * tok_rows, axis=0)
    grad_normed = lax.psum_scatter(
        contract(gate_rows, gate_all, 1, 1) + contract(upper_rows, upper_all, 1, 1),
        "ha",
        scatter_dimension=0,
        tiled=True,
    )
    tile_gate = contract(features, grad_gate, 0, 0)
    tile_upper = contract(features, grad_upper, 0, 0)
    tile_down = contract(cotangent, hidden, 0, 0)
    tiles = (
        lax.psum_scatter(
            tile_gate.astype(jnp.bfloat16), "ma", scatter_dimension=0, tiled=True
        ).astype(jnp.float32),
        lax.psum_scatter(
            tile_upper.astype(jnp.bfloat16), "ma", scatter_dimension=0, tiled=True
        ).astype(jnp.float32),
        lax.psum_scatter(
            tile_down.astype(jnp.bfloat16), "ma", scatter_dimension=0, tiled=True
        ).astype(jnp.float32),
    )
    tile_totals = (
        lax.psum(tiles[0].astype(jnp.bfloat16), "rows").astype(jnp.float32),
        lax.psum(tiles[1].astype(jnp.bfloat16), "rows").astype(jnp.float32),
        lax.psum(tiles[2].astype(jnp.bfloat16), "rows").astype(jnp.float32),
    )
    mixed_out = (h_one + branch).astype(jnp.bfloat16)
    unused_m, pull_mlp = jax.vjp(norm_rows, h_one, norm_mlp)
    grad_h_norm, grad_gain_mlp = pull_mlp(grad_normed)
    grad_h_one = grad_out.astype(jnp.float32) + grad_h_norm
    grad_attn = grad_h_one.astype(jnp.bfloat16)
    grad_wout = contract(attn_o, grad_attn, 0, 0)
    grad_o = contract(grad_attn, w_out, 1, 1).astype(jnp.bfloat16).reshape(shape_four)
    grad_qrot, grad_krot, grad_vmix = lax.map(
        attend_backward, (q_rot, k_rot, v_heads, grad_o, log_totals, lengths)
    )
    grad_vflat = grad_vmix.reshape(tok_rows, D)
    grad_first = 0.5 * grad_vflat
    grad_vlin = (0.5 * grad_vflat).astype(jnp.bfloat16)
    grad_qlin = unrotate(grad_qrot).reshape(tok_rows, D).astype(jnp.bfloat16)
    grad_klin = unrotate(grad_krot).reshape(tok_rows, D).astype(jnp.bfloat16)
    grad_normed_a = (
        contract(grad_qlin, w_query, 1, 1)
        + contract(grad_klin, w_key, 1, 1)
        + contract(grad_vlin, w_value, 1, 1)
    )
    grad_wq = contract(normed_a, grad_qlin, 0, 0)
    grad_wk = contract(normed_a, grad_klin, 0, 0)
    grad_wv = contract(normed_a, grad_vlin, 0, 0)
    unused_a, pull_attn = jax.vjp(norm_rows, inputs, norm_attn)
    grad_in_norm, grad_gain_attn = pull_attn(grad_normed_a)
    grad_tokens = grad_h_one + grad_in_norm
    summed = lax.psum(
        (grad_wq, grad_wk, grad_wv, grad_wout, grad_gain_attn, grad_gain_mlp), ("rows", "ha", "ma")
    )
    return (
        mixed_out,
        grad_tokens,
        grad_first,
        summed[0],
        summed[1],
        summed[2],
        summed[3],
        summed[4],
        summed[5],
        tile_totals[0],
        tile_totals[1],
        tile_totals[2].T,
    )


def solution(mesh):
    return jax.shard_map(
        body,
        mesh=mesh,
        in_specs=(
            P(("rows", "ha", "ma"), None),
            P(("rows", "ha", "ma"), None),
            P(("rows", "ha", "ma")),
            P(),
            P(),
            P(),
            P(),
            P(),
            P(),
            P("ma", "ha"),
            P("ma", "ha"),
            P("ha", "ma"),
            P(("rows", "ha", "ma"), None),
        ),
        out_specs=(
            P(("rows", "ha", "ma"), None),
            P(("rows", "ha", "ma"), None),
            P(("rows", "ha", "ma"), None),
            P(),
            P(),
            P(),
            P(),
            P(),
            P(),
            P("ma", "ha"),
            P("ma", "ha"),
            P("ha", "ma"),
        ),
        check_vma=False,
    )
```

profile of v0, /device:TPU:0, one launch (start us, length us, event | category | flops | bytes accessed | tf_op | source)
XLA Modules:
  0.0 1216.6 jit_solution(10065930827233244892)
XLA Ops:
  39.8 7.6 fusion.71
  47.4 8.3 fusion.6
  56.1 15.4 %fusion.70 = (f32[16,512]{1,0:T(8,128)S(1)}, f32[16,512,1024]{2,1,0:T(8,128)}) fusion(bf16[1024,16,32]{0,2,1:T(8,128)(2,1)} %bitcast.109, bf16[1024,16,32]{0,2,1:T(8,128)(2,1)} %bitcast.111, bf16[1,1024,16,32]{1,3,2,0:T(8,128)(2,1)S(1)} %get-tuple-element.180, bf16[1,1024,16,32]{1,3,2,0:T(8,128)(2,1)S(1)} %get-tuple-element.179, ...), kind=kOutput, calls=%fused_computation.123 | convolution fusion | flops 1105190912 | bytes 38305792 | tf_op jit(solution)/shard_map/while/body/eval_jaxpr/qhd,khd->hqk/dot_general | solution.py:58
  71.5 15.0 %fusion = f32[16,512]{1,0:T(8,128)S(1)} fusion(f32[16,512,1024]{2,1,0:T(8,128)} %get-tuple-element.194, f32[16,512]{1,0:T(8,128)S(1)} %get-tuple-element.193), kind=kLoop, calls=%fused_computation.6 | loop fusion | flops 16769024 | bytes 33619968 | tf_op jit(solution)/shard_map/while/body/eval_jaxpr/reduce_sum | solution.py:73
  86.6 13.9 %fusion.31 = bf16[512,16,64]{0,2,1:T(8,128)(2,1)S(1)} fusion(bf16[1024,16,64]{0,2,1:T(8,128)(2,1)S(1)} %bitcast.117, f32[16,512,1024]{2,1,0:T(8,128)} %get-tuple-element.194, f32[16,512]{1,0:T(8,128)S(1)} %fusion, f32[16,512]{1,0:T(8,128)S(1)} %get-tuple-element.193), kind=kOutput, calls=%fused_computation.82 | convolution fusion | flops 1099431936 | bytes 36765696 | tf_op jit(solution)/shard_map/while/body/eval_jaxpr/hqk,khd->qhd/dot_general | solution.py:75
  115.9 88.5 %all-gather.6.cloned.1.call-done = bf16[4096,1024]{0,1:T(8,128)(2,1)} async-done(((bf16[1024,1024]{0,1:T(8,128)(2,1)}), bf16[4096,1024]{0,1:T(8,128)(2,1)}) %all-gather.6.cloned.1.call-update) | async-done | bytes 8388624 | tf_op jit(solution)/shard_map/all_gather | solution.py:161
  204.4 12.4 %fusion.74 = f32[4096,704]{0,1:T(8,128)} fusion(bf16[1024,704]{0,1:T(8,128)(2,1)} %all-gather.10.cloned.1.call-done, bf16[4096,1024]{0,1:T(8,128)(2,1)} %all-gather.6.cloned.1.call-done), kind=kOutput, calls=%fused_computation.127 | convolution fusion | flops 5905580032 | bytes 21364736 | tf_op jit(solution)/shard_map/dot_general | solution.py:163
  216.8 24.8 %all-gather.8.cloned.1.call-done = bf16[1024,704]{0,1:T(8,128)(2,1)} async-done(((bf16[256,704]{0,1:T(8,128)(2,1)}), bf16[1024,704]{0,1:T(8,128)(2,1)}) %all-gather.8.cloned.1.call-update) | async-done | bytes 1441808 | tf_op jit(solution)/shard_map/all_gather | solution.py:157
  241.6 12.4 %fusion.73 = f32[4096,704]{0,1:T(8,128)} fusion(bf16[1024,704]{0,1:T(8,128)(2,1)} %all-gather.8.cloned.1.call-done, bf16[4096,1024]{0,1:T(8,128)(2,1)} %all-gather.6.cloned.1.call-done), kind=kOutput, calls=%fused_computation.126 | convolution fusion | flops 5905580032 | bytes 21364736 | tf_op jit(solution)/shard_map/dot_general | solution.py:162
  253.9 22.9 %all-gather.12.cloned.1.call-done = bf16[704,1024]{1,0:T(8,128)(2,1)} async-done(((bf16[704,256]{1,0:T(8,128)(2,1)}), bf16[704,1024]{1,0:T(8,128)(2,1)}) %all-gather.12.cloned.1.call-update) | async-done | bytes 1441808 | tf_op jit(solution)/shard_map/all_gather | solution.py:159
  276.8 87.6 %all-gather.14.cloned.1.call-done = bf16[4096,1024]{1,0:T(8,128)(2,1)} async-done(((bf16[1024,1024]{1,0:T(8,128)(2,1)}), bf16[4096,1024]{1,0:T(8,128)(2,1)}) %all-gather.14.cloned.1.call-update) | async-done | bytes 8388624 | tf_op jit(solution)/shard_map/all_gather | solution.py:175
  364.4 22.7 %multiply_convert_fusion.2 = (bf16[4096,704]{0,1:T(8,128)(2,1)}, bf16[4096,704]{0,1:T(8,128)(2,1)}, bf16[4096,704]{0,1:T(8,128)(2,1)}) fusion(f32[4096,704]{0,1:T(8,128)} %fusion.73, f32[4096,704]{0,1:T(8,128)} %fusion.74, bf16[4096,1024]{1,0:T(8,128)(2,1)} %all-gather.14.cloned.1.call-done, bf16[704,1024]{1,0:T(8,128)(2,1)} %all-gather.12.cloned.1.call-done), kind=kOutput, calls=%fused_computation.19 | convolution fusion | flops 5951717376 | bytes 50200576 | tf_op jit(solution)/shard_map/dot_general | solution.py:43
  387.1 11.6 convolution_convert_fusion.4
  398.8 11.5 convolution_convert_fusion.3
  410.4 11.2 fusion.30
  421.7 13.5 %fusion.72 = f32[4096,1024]{0,1:T(8,128)} fusion(bf16[4096,704]{0,1:T(8,128)(2,1)} %get-tuple-element.173, bf16[1024,704]{0,1:T(8,128)(2,1)} %all-gather.8.cloned.1.call-done), kind=kOutput, calls=%fused_computation.125 | convolution fusion | flops 5905580032 | bytes 23986176 | tf_op jit(solution)/shard_map/dot_general | solution.py:43
  435.2 15.4 %convolution_add_fusion = f32[4096,1024]{0,1:T(8,128)} fusion(f32[4096,1024]{0,1:T(8,128)} %fusion.72, bf16[4096,704]{0,1:T(8,128)(2,1)} %get-tuple-element.172, bf16[1024,704]{0,1:T(8,128)(2,1)S(1)} %copy-done.65), kind=kOutput, calls=%fused_computation.32 | convolution fusion | flops 5909774336 | bytes 40763392 | tf_op jit(solution)/shard_map/dot_general | solution.py:43
  451.9 11.7 convolution_convert_fusion
  467.8 34.0 %reduce-scatter.14.cloned.1.call-done = bf16[256,704]{0,1:T(8,128)(2,1)} async-done(((bf16[1024,704]{0,1:T(8,128)(2,1)}), bf16[256,704]{0,1:T(8,128)(2,1)}) %reduce-scatter.14.cloned.1.call-update) | async-done | bytes 360464 | tf_op jit(solution)/shard_map/reduce_scatter | solution.py:196
  501.8 155.7 %reduce-scatter.8.cloned.1.call-done = f32[1024,1024]{0,1:T(8,128)} async-done(((f32[4096,1024]{0,1:T(8,128)}), f32[1024,1024]{0,1:T(8,128)}) %reduce-scatter.8.cloned.1.call-update) | async-done | bytes 4194320 | tf_op jit(solution)/shard_map/reduce_scatter | solution.py:180
  662.7 84.2 %reduce-scatter.6.cloned.1.call-done = bf16[1024,1024]{0,1:T(8,128)(2,1)} async-done(((bf16[4096,1024]{0,1:T(8,128)(2,1)}), bf16[1024,1024]{0,1:T(8,128)(2,1)}) %reduce-scatter.6.cloned.1.call-update) | async-done | bytes 2097168 | tf_op jit(solution)/shard_map/reduce_scatter | solution.py:165
  746.9 7.1 fusion.16
  758.0 11.3 multiply_reduce_fusion.1
  769.3 12.3 %multiply_convert_fusion.1 = bf16[16,512,512]{1,2,0:T(8,128)(2,1)S(1)} fusion(f32[16,512,512]{1,2,0:T(8,128)} %get-tuple-element.200, f32[16,512,512]{1,2,0:T(8,128)} %get-tuple-element.196, f32[16,512]{1,0:T(8,128)S(1)} %get-tuple-element.199, f32[16,512]{1,0:T(8,128)S(1)} %log_add_fusion.1), kind=kLoop, calls=%fused_computation.10 | loop fusion | flops 16777216 | bytes 42008576 | tf_op jit(solution)/shard_map/while/body/eval_jaxpr/convert_element_type | solution.py:101
  788.5 9.9 fusion.25
  802.8 22.2 %multiply_reduce_fusion = (f32[16,512]{1,0:T(8,128)S(1)}, f32[16,512,1024]{2,1,0:T(8,128)}) fusion(f32[16,512,1024]{2,1,0:T(8,128)} %get-tuple-element.194, f32[16,512]{1,0:T(8,128)S(1)} %log_add_fusion, bf16[512,16,64]{0,2,1:T(8,128)(2,1)S(1)} %bitcast.113, bf16[1024,16,64]{0,2,1:T(8,128)(2,1)S(1)} %bitcast.118), kind=kOutput, calls=%fused_computation.1 | convolution fusion | flops 1098899456 | bytes 70320128 | tf_op jit(solution)/shard_map/while/body/eval_jaxpr/qhd,khd->hqk/dot_general | solution.py:95
  825.0 27.9 %multiply_convert_fusion = bf16[16,512,1024]{2,1,0:T(8,128)(2,1)} fusion(f32[16,512,1024]{2,1,0:T(8,128)} %get-tuple-element.202, f32[16,512,1024]{2,1,0:T(8,128)} %get-tuple-element.194, f32[16,512]{1,0:T(8,128)S(1)} %get-tuple-element.201, f32[16,512]{1,0:T(8,128)S(1)} %log_add_fusion), kind=kLoop, calls=%fused_computation | loop fusion | flops 33554432 | bytes 83951616 | tf_op jit(solution)/shard_map/while/body/eval_jaxpr/convert_element_type | solution.py:101
  852.9 12.9 %multiply_bitcast_fusion.1 = f32[512,16,64]{0,2,1:T(8,128)} fusion(bf16[16,512,1024]{2,1,0:T(8,128)(2,1)} %multiply_convert_fusion, bf16[1024,16,32]{0,2,1:T(8,128)(2,1)} %bitcast.110, bf16[1024,16,32]{0,2,1:T(8,128)(2,1)} %bitcast.112), kind=kOutput, calls=%fused_computation.66 | convolution fusion | flops 1078460416 | bytes 20971520 | tf_op jit(solution)/shard_map/while/body/eval_jaxpr/hqk,khd->qhd/dot_general | solution.py:103
  865.8 11.6 fusion.21
  877.4 16.5 %fusion.20 = f32[1024,16,64]{0,2,1:T(8,128)} fusion(f32[512,16,64]{0,2,1:T(8,128)} %fusion.25, bf16[512,16,64]{0,2,1:T(8,128)(2,1)} %bitcast.114, f32[16,512,1024]{2,1,0:T(8,128)} %get-tuple-element.194, f32[16,512]{1,0:T(8,128)S(1)} %log_add_fusion), kind=kOutput, calls=%fused_computation.45 | convolution fusion | flops 1092616192 | bytes 40927232 | tf_op jit(solution)/shard_map/while/body/eval_jaxpr/hqk,qhd->khd/dot_general | solution.py:113
  948.7 41.1 %all-reduce.6 = (f32[1024]{0:T(1024)}, f32[1024]{0:T(1024)}) all-reduce(f32[1024]{0:T(1024)S(1)} %get-tuple-element.161, f32[1024]{0:T(1024)S(1)} %copy-done.56), channel_id=1, replica_groups=mesh['rows'=2,'ha'=4,'ma'=4] {'rows','ha','ma'}, use_global_device_ids=true, to_apply=%region_17.18 | all-reduce | flops 2048 | bytes 16384 | tf_op jit(solution)/shard_map/psum | solution.py:231
  989.8 205.1 %all-reduce.12.cloned.1.call-done = (f32[1024,1024]{1,0:T(8,128)}, f32[1024,1024]{1,0:T(8,128)}, f32[1024,1024]{1,0:T(8,128)}, f32[1024,1024]{1,0:T(8,128)}) async-done(((f32[1024,1024]{1,0:T(8,128)}, f32[1024,1024]{1,0:T(8,128)}, f32[1024,1024]{1,0:T(8,128)}, f32[1024,1024]{1,0:T(8,128)}), (f32[1024,1024]{1,0:T(8,128)}, f32[1024,1024]{1,0:T(8,128)}, f32[1024,1024]{1,0:T(8,128)}, ...) | async-done | bytes 16777232 | tf_op jit(solution)/shard_map/psum | solution.py:231
  (223 shorter events, 142.2 us)
Async XLA Ops:
  7.2 24.3 %copy-start = (bf16[1024,1024]{1,0:T(8,128)(2,1)S(1)}, bf16[1024,1024]{1,0:T(8,128)(2,1)}, u32[]{:S(2)}) copy-start(bf16[1024,1024]{1,0:T(8,128)(2,1)} %param.30) | copy-start | bytes 6291460
  7.2 108.7 %all-gather.10.cloned.1.call-start = ((), (), s32[]{:S(2)}) async-start(), calls=%async_computation.7 | async-start | bytes 1802240 | tf_op jit(solution)/shard_map/all_gather | solution.py:158
  7.9 196.5 %all-gather.6.cloned.1.call-start = ((), (), s32[]{:S(2)}) async-start(), calls=%async_computation.5 | async-start | bytes 10485760 | tf_op jit(solution)/shard_map/all_gather | solution.py:161
  14.6 16.8 %copy-start.54 = (f32[1024]{0:T(1024)}, f32[1024]{0:T(1024)S(1)}, u32[]{:S(2)}) copy-start(f32[1024]{0:T(1024)S(1)} %fusion.50) | copy-start | bytes 12292
  39.8 16.3 %copy-start.8 = (bf16[1,1024,16,32]{1,3,2,0:T(8,128)(2,1)}, bf16[1,1024,16,32]{1,3,2,0:T(8,128)(2,1)S(1)}, u32[]{:S(2)}) copy-start(bf16[1,1024,16,32]{1,3,2,0:T(8,128)(2,1)S(1)} %get-tuple-element.179) | copy-start | bytes 3145732
  39.8 16.3 %copy-start.10 = (bf16[1,1024,16,32]{1,3,2,0:T(8,128)(2,1)}, bf16[1,1024,16,32]{1,3,2,0:T(8,128)(2,1)S(1)}, u32[]{:S(2)}) copy-start(bf16[1,1024,16,32]{1,3,2,0:T(8,128)(2,1)S(1)} %get-tuple-element.180) | copy-start | bytes 3145732
  47.4 53.1 %copy-start.40 = (f32[16,512]{1,0:T(8,128)}, f32[16,512]{1,0:T(8,128)S(1)}, u32[]{:S(2)}) copy-start(f32[16,512]{1,0:T(8,128)S(1)} %get-tuple-element.195) | copy-start | bytes 98308
  55.7 44.8 %copy-start.44 = (f32[16,512]{1,0:T(8,128)}, f32[16,512]{1,0:T(8,128)S(1)}, u32[]{:S(2)}) copy-start(f32[16,512]{1,0:T(8,128)S(1)} %fusion.6) | copy-start | bytes 98308
  71.5 15.1 %copy-start.42 = (f32[16,512]{1,0:T(8,128)}, f32[16,512]{1,0:T(8,128)S(1)}, u32[]{:S(2)}) copy-start(f32[16,512]{1,0:T(8,128)S(1)} %get-tuple-element.193) | copy-start | bytes 98308
  71.5 15.1 %copy-start.22 = (bf16[1024,1024]{0,1:T(8,128)(2,1)S(1)}, bf16[1024,1024]{0,1:T(8,128)(2,1)}, u32[]{:S(2)}) copy-start(bf16[1024,1024]{0,1:T(8,128)(2,1)} %copy-done.21) | copy-start | bytes 6291460
  71.5 29.0 %slice-start = ((s8[16777216]{0:T(1024)(128)(4,1)}), s8[4194304]{0:T(1024)(128)(4,1)S(1)}, s32[]{:S(2)}) async-start(s8[16777216]{0:T(1024)(128)(4,1)} %bitcast.104), calls=%async_computation.17 | async-start | bytes 8388608
  86.5 14.0 %copy-start.46 = (f32[16,512]{1,0:T(8,128)}, f32[16,512]{1,0:T(8,128)S(1)}, u32[]{:S(2)}) copy-start(f32[16,512]{1,0:T(8,128)S(1)} %fusion) | copy-start | bytes 98308
  86.6 14.0 %slice-start.1 = ((s8[16777216]{0:T(1024)(128)(4,1)}), s8[4194304]{0:T(1024)(128)(4,1)S(1)}, s32[]{:S(2)}) async-start(s8[16777216]{0:T(1024)(128)(4,1)} %bitcast.104), calls=%async_computation.18 | async-start | bytes 8388608
  86.6 14.0 %slice-start.2 = ((s8[16777216]{0:T(1024)(128)(4,1)}), s8[4194304]{0:T(1024)(128)(4,1)S(1)}, s32[]{:S(2)}) async-start(s8[16777216]{0:T(1024)(128)(4,1)} %bitcast.104), calls=%async_computation.19 | async-start | bytes 8388608
  86.6 14.2 %slice-start.3 = ((s8[16777216]{0:T(1024)(128)(4,1)}), s8[4194304]{0:T(1024)(128)(4,1)S(1)}, s32[]{:S(2)}) async-start(s8[16777216]{0:T(1024)(128)(4,1)} %bitcast.104), calls=%async_computation.20 | async-start | bytes 8388608
  86.6 14.4 %copy-start.26 = (bf16[512,1024]{0,1:T(8,128)(2,1)S(1)}, bf16[512,1024]{0,1:T(8,128)(2,1)}, u32[]{:S(2)}) copy-start(bf16[512,1024]{0,1:T(8,128)(2,1)} %slice.181) | copy-start | bytes 3145732
  114.0 127.6 %all-gather.8.cloned.1.call-start = ((), (), s32[]{:S(2)}) async-start(), calls=%async_computation.6 | async-start | bytes 1802240 | tf_op jit(solution)/shard_map/all_gather | solution.py:157
  114.7 162.1 %all-gather.12.cloned.1.call-start = ((), (), s32[]{:S(2)}) async-start(), calls=%async_computation.8 | async-start | bytes 1802240 | tf_op jit(solution)/shard_map/all_gather | solution.py:159
  115.3 249.1 %all-gather.14.cloned.1.call-start = ((), (), s32[]{:S(2)}) async-start(), calls=%async_computation.10 | async-start | bytes 10485760 | tf_op jit(solution)/shard_map/all_gather | solution.py:175
  115.9 351.9 %reduce-scatter.10.cloned.1.call-start = ((), (), s32[]{:S(2)}) async-start(), calls=%async_computation.12 | async-start | bytes 1802240 | tf_op jit(solution)/shard_map/reduce_scatter | solution.py:190
  398.8 69.0 %reduce-scatter.12.cloned.1.call-start = ((), (), s32[]{:S(2)}) async-start(), calls=%async_computation.13 | async-start | bytes 1802240 | tf_op jit(solution)/shard_map/reduce_scatter | solution.py:193
  410.3 91.4 %reduce-scatter.14.cloned.1.call-start = ((), (), s32[]{:S(2)}) async-start(), calls=%async_computation.14 | async-start | bytes 1802240 | tf_op jit(solution)/shard_map/reduce_scatter | solution.py:196
  421.6 236.0 %reduce-scatter.8.cloned.1.call-start = ((), (), s32[]{:S(2)}) async-start(), calls=%async_computation.11 | async-start | bytes 20971520 | tf_op jit(solution)/shard_map/reduce_scatter | solution.py:180
  450.6 296.3 %reduce-scatter.6.cloned.1.call-start = ((), (), s32[]{:S(2)}) async-start(), calls=%async_computation.9 | async-start | bytes 10485760 | tf_op jit(solution)/shard_map/reduce_scatter | solution.py:165
  463.6 193.9 %copy-start.49 = (f32[1024]{0:T(1024)S(1)}, f32[1024]{0:T(1024)}, u32[]{:S(2)}) copy-start(f32[1024]{0:T(1024)} %copy-done.48) | copy-start | bytes 12292
  463.7 193.9 %copy-start.51 = (f32[1024]{0:T(1024)S(1)}, f32[1024]{0:T(1024)}, u32[]{:S(2)}) copy-start(f32[1024]{0:T(1024)} %param.33) | copy-start | bytes 12292
  463.7 450.1 %all-reduce.14.cloned.1.call-start = ((), (), s32[]{:S(2)}) async-start(), calls=%async_computation.16 | async-start | bytes 2162688 | tf_op jit(solution)/shard_map/psum | solution.py:201
  501.8 160.9 %copy-start.58 = (f32[1024]{0:T(1024)S(1)}, f32[1024]{0:T(1024)}, u32[]{:S(2)}) copy-start(f32[1024]{0:T(1024)} %copy-done.57) | copy-start | bytes 12292
  501.8 693.1 %all-reduce.12.cloned.1.call-start = ((), (), s32[]{:S(2)}) async-start(), calls=%async_computation.15 | async-start | bytes 33554432 | tf_op jit(solution)/shard_map/psum | solution.py:231
  754.0 44.3 %copy-start.16 = (f32[1024,1024]{0,1:T(8,128)}, f32[1024,1024]{0,1:T(8,128)S(1)}, u32[]{:S(2)}) copy-start(f32[1024,1024]{0,1:T(8,128)S(1)} %get-tuple-element.183) | copy-start | bytes 12582916
  756.5 46.2 %copy-start.20 = (bf16[512,1024]{0,1:T(8,128)(2,1)}, bf16[512,1024]{0,1:T(8,128)(2,1)S(1)}, u32[]{:S(2)}) copy-start(bf16[512,1024]{0,1:T(8,128)(2,1)S(1)} %get-tuple-element.186) | copy-start | bytes 3145732
  877.4 16.5 %copy-start.19 = (f32[512,16,64]{0,2,1:T(8,128)S(1)}, f32[512,16,64]{0,2,1:T(8,128)}, u32[]{:S(2)}) copy-start(f32[512,16,64]{0,2,1:T(8,128)} %multiply_bitcast_fusion.2) | copy-start | bytes 6291460
  (51 other events, 245.3 us)
Sparse Core Ops, SparseCore 0:
  9.6 38.2 all-gather.9
  114.1 90.2 all-gather.5
  206.0 35.5 all-gather.7
  243.0 33.7 all-gather.11
  278.5 85.8 all-gather.13
  398.9 33.2 reduce-scatter.9
  435.1 32.1 reduce-scatter.11
  469.6 32.1 reduce-scatter.13
  504.8 152.7 reduce-scatter.7
  660.5 86.3 reduce-scatter.5
  749.6 19.7 all-reduce.13
  913.9 280.9 all-reduce.11
where the time goes:
time: 1230 us; the launch traced here: 1220 us
  waiting for transfers between devices  705 us (57%)
  matrix products  303 us (25%)
  other arithmetic  95.9 us (8%)
  local copies, waits for them, and re-layouts  54.2 us (4%)
  blocking collectives  41.1 us (3%)
  between operations  16.2 us (1%)
    psum x1, waiting for transfers between devices, body(): lax.psum((grad_wq, grad_wk, grad_wv, grad_wout, grad_gain_attn, grad_gain...  205 us
    reduce_scatter x1, waiting for transfers between devices, body(): lax.psum_scatter(contract(gate_rows, gate_all, 1, 1) + contract(upper_row...  156 us
    dot_general x14, matrix products, contract(): lax.dot_general(left, right, (((left_dim,), (right_dim,)), ((), ())), pre...  116 us
    all_gather x1, waiting for transfers between devices, body(): features = lax.all_gather(normed_m, 'ha', axis=0, tiled=True)  88.5 us
    all_gather x1, waiting for transfers between devices, body(): cotangent = lax.all_gather(grad_out, 'ha', axis=0, tiled=True)  87.6 us
    reduce_scatter x1, waiting for transfers between devices, body(): lax.psum_scatter(jnp.dot(lax.slice_in_dim(hidden, 0, lax.axis_size('ha')...  84.2 us
    unnamed x152, local copies, waits for them, and re-layouts  52.9 us
    psum x1, blocking collectives, body(): lax.psum((grad_wq, grad_wk, grad_wv, grad_wout, grad_gain_attn, grad_gain...  41.1 us
  transfers between devices with their start and end apart: 12, of which 8 were waited for; matrix products, arithmetic and copies ran while one was open for 32% of the time, Pallas kernels for 0%

commit v1 on v0

v1 whole, which is shorter than its diff:
```python
import functools
import math

import jax
import jax.numpy as jnp
import numpy as np
from jax import lax
from jax.experimental import pallas as pl
from jax.experimental.pallas import tpu as pltpu
from jax.sharding import PartitionSpec as P

D = 1024
H = 16
HD = 64
SLOT = 1024
EPS = 1e-06
GROUP = 4
GW = GROUP * HD
QB = 256
SCALE = 1.0 / math.sqrt(HD)
C2 = SCALE * math.log2(math.e)
F32 = jnp.float32
BF16 = jnp.bfloat16
MIB = 1 << 20


def nn(a, b):
    return lax.dot_general(a, b, (((1,), (0,)), ((), ())), preferred_element_type=F32)


def nt(a, b):
    return lax.dot_general(a, b, (((1,), (1,)), ((), ())), preferred_element_type=F32)


def tn(a, b):
    return lax.dot_general(a, b, (((0,), (0,)), ((), ())), preferred_element_type=F32)


def rope_tables():
    place = np.arange(SLOT, dtype=np.float32)
    frequency = np.float32(10000.0) ** (-np.arange(HD // 2, dtype=np.float32) * np.float32(2.0) / np.float32(HD))
    angles = place[:, None] * frequency[None, :]
    cosine, sine = np.cos(angles), np.sin(angles)
    cos_row = np.concatenate([cosine] * 4, axis=1)
    sin_row = np.concatenate([-sine, sine, -sine, sine], axis=1)
    return cos_row.astype(np.float32), sin_row.astype(np.float32)


def lanes(shape):
    return lax.broadcasted_iota(jnp.int32, shape, 1)


def partner(v):
    first = (lanes(v.shape) & 63) < 32
    return jnp.where(first, pltpu.roll(v, 96, 1), pltpu.roll(v, 32, 1))


def turn(v, cos, sin):
    parts = []
    for at in range(0, v.shape[1], 128):
        piece = v[:, at : at + 128]
        parts.append(piece * cos + partner(piece) * sin)
    return jnp.concatenate(parts, axis=1)


def low3(v):
    hi = v.astype(BF16).astype(F32)
    rest = v - hi
    mid = rest.astype(BF16).astype(F32)
    return hi, mid, rest - mid


def fwd_kernel(
    len_ref, x_ref, gain_ref, wq_ref, wk_ref, wv_ref, fv_ref, cos_ref, sin_ref, wo_ref, gain_m_ref,
    q_ref, k_ref, v_ref, o_ref, st_ref, nma_ref, h1_ref, nmm_ref,
):
    g = pl.program_id(0)

    @pl.when(g == 0)
    def _():
        x = x_ref[...].astype(F32)
        r = lax.rsqrt(jnp.mean(x * x, axis=-1, keepdims=True) + EPS)
        nma_ref[...] = (x * r * gain_ref[...]).astype(BF16)
        h1_ref[...] = x
        st_ref[...] = jnp.zeros_like(st_ref)

    nm = nma_ref[...]
    cos, sin = cos_ref[...], sin_ref[...]
    q_ref[...] = turn(nn(nm, wq_ref[...]), cos, sin).astype(BF16)
    k_ref[...] = turn(nn(nm, wk_ref[...]), cos, sin).astype(BF16)
    v_ref[...] = (0.5 * nn(nm, wv_ref[...]) + 0.5 * fv_ref[...].astype(F32)).astype(BF16)
    length = len_ref[0]
    tile = (SLOT, 128)
    lane = lanes(tile)
    row = lax.broadcasted_iota(jnp.int32, tile, 0)
    k_extra = jnp.where((lane == 0) & (row >= length), -1e30, 0.0).astype(BF16)
    q_extra = jnp.where(lane == 0, 1.0, 0.0).astype(BF16)
    ones = jnp.ones(tile, BF16)
    low_lane = lane < HD
    qlane = lanes((QB, 128))
    causal = lax.broadcasted_iota(jnp.int32, (QB, QB), 1) <= lax.broadcasted_iota(jnp.int32, (QB, QB), 0)
    for pair in range(GROUP // 2):
        cols = pl.ds(pair * 128, 128)
        qp, kp, vp = q_ref[:, cols], k_ref[:, cols], v_ref[:, cols]
        q_ext = jnp.concatenate([qp, q_extra], axis=1)
        k_exts, v_exts = [], []
        for e in range(2):
            mine = low_lane if e == 0 else ~low_lane
            k_exts.append(jnp.concatenate([jnp.where(mine, kp, 0), k_extra], axis=1))
            v_exts.append(jnp.concatenate([jnp.where(mine, vp, 0), ones], axis=1))
        for qb in range(SLOT // QB):
            rows = slice(qb * QB, (qb + 1) * QB)
            top = (qb + 1) * QB
            out = None
            stats = st_ref[rows, :].astype(F32)
            for e in range(2):
                s = nt(q_ext[rows], k_exts[e][:top])
                diag = jnp.where(causal, s[:, top - QB :], -1e30)
                s = diag if qb == 0 else jnp.concatenate([s[:, : top - QB], diag], axis=1)
                m = jnp.max(s, axis=-1, keepdims=True)
                p = jnp.exp2((s - m) * C2).astype(BF16)
                res = nn(p, v_exts[e][:top])
                total = res[:, 128:]
                part = res[:, :128] / total
                out = part if out is None else out + part
                hi, mid, rest = low3(m + jnp.log2(total) * (1.0 / C2))
                base = 8 * (g * GROUP + pair * 2 + e)
                stats = jnp.where(qlane == base, hi, stats)
                stats = jnp.where(qlane == base + 1, mid, stats)
                stats = jnp.where(qlane == base + 2, rest, stats)
                stats = jnp.where(qlane == base + 3, 1.0, stats)
            o_ref[rows, cols] = out.astype(BF16)
            st_ref[rows, :] = stats.astype(BF16)
    h1_ref[...] += nn(o_ref[...], wo_ref[...])

    @pl.when(g == pl.num_programs(0) - 1)
    def _():
        h = h1_ref[...]
        r = lax.rsqrt(jnp.mean(h * h, axis=-1, keepdims=True) + EPS)
        nmm_ref[...] = (h * r * gain_m_ref[...]).astype(BF16)


def attention_forward(length, x, gain, wq, wk, wv, fv, cos, sin, wo, gain_m):
    whole = lambda *_: (0, 0)
    col = lambda g, *_: (0, g)
    tok = x.shape[0]
    full = pl.BlockSpec((tok, D), whole)
    blk = pl.BlockSpec((tok, GW), col)
    wblk = pl.BlockSpec((D, GW), col)
    vec = pl.BlockSpec((1, D), whole)
    tab = pl.BlockSpec((tok, 128), whole)
    sds = jax.ShapeDtypeStruct
    return pl.pallas_call(
        fwd_kernel,
        grid_spec=pltpu.PrefetchScalarGridSpec(
            num_scalar_prefetch=1,
            grid=(H // GROUP,),
            in_specs=[full, vec, wblk, wblk, wblk, blk, tab, tab, pl.BlockSpec((GW, D), lambda g, *_: (g, 0)), vec],
            out_specs=[blk, blk, blk, blk, tab, full, full, full],
        ),
        out_shape=[sds((tok, D), BF16)] * 4 + [sds((tok, 128), BF16), sds((tok, D), BF16), sds((tok, D), F32), sds((tok, D), BF16)],
        compiler_params=pltpu.CompilerParams(vmem_limit_bytes=56 * MIB),
        cost_estimate=pl.CostEstimate(flops=30 * 10**9, bytes_accessed=40 * 10**6, transcendentals=10**7),
        name="attention_forward",
    )(length, x, gain, wq, wk, wv, fv, cos, sin, wo, gain_m)


def prep_kernel(n, order_ref, nma_ref, o_ref, nmm_ref, dy_ref, nmat_ref, ot_ref, nmmt_ref, dyt_ref, buf):
    nmmt_ref[...] = nmm_ref[...].T
    dyt_ref[...] = dy_ref[...].T
    size = D // n
    for src, dst in ((nma_ref, nmat_ref), (o_ref, ot_ref)):
        if n == 1:
            dst[...] = src[...].T
        else:
            buf[...] = src[...].T
            for i in range(n):
                dst[pl.ds(i * size, size), :] = buf[pl.ds(pl.multiple_of(order_ref[i] * size, size), size), :]


def prepare(order, n, nma, o, nmm, dy):
    vm = pl.BlockSpec(memory_space=pltpu.VMEM)
    return pl.pallas_call(
        functools.partial(prep_kernel, n),
        in_specs=[pl.BlockSpec(memory_space=pltpu.SMEM)] + [vm] * 4,
        out_specs=[vm] * 4,
        out_shape=[jax.ShapeDtypeStruct((D, dy.shape[0]), BF16)] * 4,
        scratch_shapes=[pltpu.VMEM((D, dy.shape[0]), BF16)],
        compiler_params=pltpu.CompilerParams(vmem_limit_bytes=30 * MIB),
        cost_estimate=pl.CostEstimate(flops=10**9, bytes_accessed=16 * 10**6, transcendentals=0),
        name="prepare",
    )(order, nma, o, nmm, dy)


def wout_kernel(ot_ref, da_ref, mine_ref, other_ref):
    mine_ref[...] = nn(ot_ref[: D // 2, :], da_ref[...]).astype(BF16)
    other_ref[...] = nn(ot_ref[D // 2 :, :], da_ref[...]).astype(BF16)


def wout_grad(ot, da):
    vm = pl.BlockSpec(memory_space=pltpu.VMEM)
    return pl.pallas_call(
        wout_kernel,
        in_specs=[vm] * 2,
        out_specs=[vm] * 2,
        out_shape=[jax.ShapeDtypeStruct((D // 2, D), BF16)] * 2,
        compiler_params=pltpu.CompilerParams(vmem_limit_bytes=30 * MIB),
        cost_estimate=pl.CostEstimate(flops=2 * 10**9, bytes_accessed=6 * 10**6, transcendentals=0),
        name="wout_grad",
    )(ot, da)


def bwd_kernel(
    first_group, len_ref, da_ref, wo_ref, q_ref, k_ref, v_ref, o_ref, st_ref, nmt_ref, cos_ref, sin_ref,
    dq_ref, dk_ref, dv_ref, gf_ref, mine_ref, other_ref, dq_acc,
):
    g = pl.program_id(0) + first_group
    do_all = nt(da_ref[...], wo_ref[...]).astype(BF16)
    prod = do_all.astype(F32) * o_ref[...].astype(F32)
    hi = prod.astype(BF16)
    lo = (prod - hi.astype(F32)).astype(BF16)
    sel_row = lax.broadcasted_iota(jnp.int32, (GW, 128), 0) // HD + g * GROUP
    sel_lane = lanes((GW, 128))
    pick = jnp.where((sel_lane // 8 == sel_row) & ((sel_lane & 7) >= 4) & ((sel_lane & 7) <= 5), 1.0, 0.0).astype(BF16)
    delta = nn(hi, pick) + nn(lo, pick)
    tile = (SLOT, 128)
    lane = lanes(tile)
    d_hi = delta.astype(BF16)
    d_ext = jnp.where((lane & 7) == 4, d_hi.astype(F32), delta - d_hi.astype(F32)).astype(BF16)
    length = len_ref[0]
    row = lax.broadcasted_iota(jnp.int32, tile, 0)
    dead = row >= length
    low_lane = lane < HD
    st = st_ref[...]
    visible = lax.broadcasted_iota(jnp.int32, (QB, QB), 0) <= lax.broadcasted_iota(jnp.int32, (QB, QB), 1)
    dq_acc[...] = jnp.zeros_like(dq_acc)
    for pair in range(GROUP // 2):
        cols = pl.ds(pair * 128, 128)
        qp, kp, vp = q_ref[:, cols], k_ref[:, cols], v_ref[:, cols]
        dop = do_all[:, pair * 128 : pair * 128 + 128]
        q_ext = jnp.concatenate([qp, st], axis=1)
        do_ext = jnp.concatenate([dop, d_ext], axis=1)
        heads = []
        for e in range(2):
            mine = low_lane if e == 0 else ~low_lane
            at = lane - 8 * (g * GROUP + pair * 2 + e)
            k_x = jnp.where((at >= 0) & (at < 3), -1.0, jnp.where((at == 3) & dead, -1e30, 0.0)).astype(BF16)
            v_x = jnp.where((at >= 4) & (at < 6), -1.0, 0.0).astype(BF16)
            k_m = jnp.where(mine, kp, 0)
            heads.append((
                k_m,
                jnp.concatenate([k_m, k_x], axis=1),
                jnp.concatenate([jnp.where(mine, vp, 0), v_x], axis=1),
                jnp.where(mine, qp, 0),
                jnp.where(mine, dop, 0),
            ))
        for kb in range(SLOT // QB):
            rows = slice(kb * QB, (kb + 1) * QB)
            start = kb * QB
            dk = dv = None
            for k_m, k_ext, v_ext, q_m, do_m in heads:
                st_ = nt(k_ext[rows], q_ext[start:])
                dp = nt(v_ext[rows], do_ext[start:])
                p = jnp.exp2(st_ * C2)
                diag = jnp.where(visible, p[:, :QB], 0.0)
                p = diag if kb == SLOT // QB - 1 else jnp.concatenate([diag, p[:, QB:]], axis=1)
                ds = (p * dp).astype(BF16)
                p = p.astype(BF16)
                dv_e = nn(p, do_m[start:])
                dk_e = nn(ds, q_m[start:])
                dk = dk_e if dk is None else dk + dk_e
                dv = dv_e if dv is None else dv + dv_e
                dq_acc[start:, cols] += tn(ds, k_m[rows])
            dk = dk * SCALE
            cos, sin = cos_ref[rows, :], sin_ref[rows, :]
            dk_ref[rows, cols] = (dk * cos - partner(dk) * sin).astype(BF16)
            half = 0.5 * dv
            gf_ref[rows, cols] = half
            dv_ref[rows, cols] = half.astype(BF16)
    cos, sin = cos_ref[...], sin_ref[...]
    for pair in range(GROUP // 2):
        cols = pl.ds(pair * 128, 128)
        dq = dq_acc[:, cols] * SCALE
        dq_ref[:, cols] = (dq * cos - partner(dq) * sin).astype(BF16)
    nmt = nmt_ref[...]
    for j, ref in enumerate((dq_ref, dk_ref, dv_ref)):
        grad = nn(nmt, ref[...]).astype(BF16)
        mine_ref[j] = grad[: D // 2]
        other_ref[j] = grad[D // 2 :]


def attention_backward(first_group, groups, length, da, wo, q, k, v, o, st, nmt, cos, sin):
    whole = lambda *_: (0, 0)
    tok = da.shape[0]
    full = pl.BlockSpec((tok, D), whole)
    blk_in = pl.BlockSpec((tok, GW), lambda g, *_: (0, g + first_group))
    blk = pl.BlockSpec((tok, GW), lambda g, *_: (0, g))
    tab = pl.BlockSpec((tok, 128), whole)
    sds = jax.ShapeDtypeStruct
    width = groups * GW
    return pl.pallas_call(
        functools.partial(bwd_kernel, first_group),
        grid_spec=pltpu.PrefetchScalarGridSpec(
            num_scalar_prefetch=1,
            grid=(groups,),
            in_specs=[full, pl.BlockSpec((GW, D), lambda g, *_: (g + first_group, 0)), blk_in, blk_in, blk_in, blk_in, tab, pl.BlockSpec((D, tok), whole), tab, tab],
            out_specs=[blk, blk, blk, blk] + [pl.BlockSpec((3, D // 2, GW), lambda g, *_: (0, 0, g))] * 2,
            scratch_shapes=[pltpu.VMEM((tok, GW), F32)],
        ),
        out_shape=[sds((tok, width), BF16)] * 3 + [sds((tok, width), F32)] + [sds((3, D // 2, width), BF16)] * 2,
        compiler_params=pltpu.CompilerParams(vmem_limit_bytes=56 * MIB),
        cost_estimate=pl.CostEstimate(flops=10 * 10**9 * groups, bytes_accessed=10 * 10**6, transcendentals=groups * 3 * 10**6),
        name="attention_backward",
    )(length, da, wo, q, k, v, o, st, nmt, cos, sin)


def sig(v):
    return 1.0 / (1.0 + jnp.exp(-v))


def mlp_kernel(nc, nz, zs_ref, *refs):
    pieces = refs[: nc * nz]
    nmt_ref, dyt_ref, nm_ref, dy_ref, h_ref, dg_ref, du_ref = refs[nc * nz : nc * nz + 7]
    outs = refs[nc * nz + 7 :]
    fs = pieces[0].shape[1]
    dz = pieces[0].shape[2]
    starts = [pl.multiple_of(zs_ref[s] * dz, dz) for s in range(nz)]
    for c in range(nc):
        gate = up = dh = None
        for s in range(nz):
            w_ref = pieces[c * nz + s]
            at = pl.ds(starts[s], dz)
            nmt, dyt = nmt_ref[at, :], dyt_ref[at, :]
            parts = nn(w_ref[0], nmt), nn(w_ref[1], nmt), nn(w_ref[2], dyt)
            gate, up, dh = parts if gate is None else (gate + parts[0], up + parts[1], dh + parts[2])
        sg = sig(gate)
        silu = gate * sg
        rows = pl.ds(c * fs, fs)
        h = (silu * up).astype(BF16)
        dg = (dh * up * (sg * (1.0 + gate * (1.0 - sg)))).astype(BF16)
        du = (dh * silu).astype(BF16)
        h_ref[rows, :], dg_ref[rows, :], du_ref[rows, :] = h, dg, du
        for s in range(nz):
            at = pl.ds(starts[s], dz)
            nm, dy = nm_ref[:, at], dy_ref[:, at]
            outs[c][s, 0] = nn(dg, nm).astype(BF16)
            outs[c][s, 1] = nn(du, nm).astype(BF16)
            outs[c][s, 2] = nn(h, dy).astype(BF16)


def mlp_block(zs, pieces, nmt, dyt, nm, dy):
    nc, nz = len(pieces), len(pieces[0])
    _, fs, dz = pieces[0][0].shape
    tok = nm.shape[0]
    sds = jax.ShapeDtypeStruct
    vm = pl.BlockSpec(memory_space=pltpu.VMEM)
    return pl.pallas_call(
        functools.partial(mlp_kernel, nc, nz),
        in_specs=[pl.BlockSpec(memory_space=pltpu.SMEM)] + [vm] * (nc * nz + 4),
        out_specs=[vm] * (3 + nc),
        out_shape=[sds((nc * fs, tok), BF16)] * 3 + [sds((nz, 3, fs, dz), BF16)] * nc,
        compiler_params=pltpu.CompilerParams(vmem_limit_bytes=44 * MIB),
        cost_estimate=pl.CostEstimate(flops=12 * nc * fs * D * tok, bytes_accessed=15 * 10**6, transcendentals=nc * fs * tok),
        name="mlp_block",
    )(zs, *[p for c in pieces for p in c], nmt, dyt, nm, dy)


def norm_back(v, gain, grad):
    ms = jnp.mean(v * v, axis=-1, keepdims=True) + EPS
    r = lax.rsqrt(ms)
    gg = grad * gain
    inner = jnp.mean(gg * v, axis=-1, keepdims=True)
    dv = r * gg - v * (inner * r * r * r)
    dgain = jnp.sum(grad * v * r, axis=0, keepdims=True)
    return dv, dgain


def mlp_out_kernel(nk, nc, nz, zs_ref, *refs):
    nw = nk * nc * nz
    pieces = refs[:nw]
    hs, dgs, dus = refs[nw : nw + nk], refs[nw + nk : nw + 2 * nk], refs[nw + 2 * nk : nw + 3 * nk]
    h1_ref, gain_ref, dy_ref, mixed_ref, dh1_ref, da_ref, dgain_ref, branch_ref, dnm_ref = refs[nw + 3 * nk :]
    fs, dz = pieces[0].shape[1:]
    i = pl.program_id(0)
    for s in range(nz):
        b = d = None
        for k in range(nk):
            for c in range(nc):
                w_ref = pieces[(k * nc + c) * nz + s]
                rows = pl.ds(c * fs, fs)
                b_one = tn(hs[k][rows, :], w_ref[2])
                d_one = tn(dgs[k][rows, :], w_ref[0]) + tn(dus[k][rows, :], w_ref[1])
                b, d = (b_one, d_one) if b is None else (b + b_one, d + d_one)
        at = pl.ds(pl.multiple_of(zs_ref[s] * dz, dz), dz)
        branch_ref[:, at] = b
        dnm_ref[:, at] = d
    h1 = h1_ref[...]
    mixed_ref[...] = (h1 + branch_ref[...]).astype(BF16)
    dv, dgain = norm_back(h1, gain_ref[...], dnm_ref[...])
    dh1 = dy_ref[...].astype(F32) + dv
    dh1_ref[...] = dh1
    da_ref[...] = dh1.astype(BF16)

    @pl.when(i == 0)
    def _():
        dgain_ref[...] = jnp.zeros_like(dgain_ref)

    dgain_ref[...] += dgain


def mlp_out(zs, blocks, hs, dgs, dus, h1, gain, dy):
    nk, nc, nz = len(blocks), len(blocks[0]), len(blocks[0][0])
    flat = [p for pieces in blocks for c in pieces for p in c]
    tok = h1.shape[0]
    tile = 256
    wspec = pl.BlockSpec(memory_space=pltpu.VMEM)
    hspec = pl.BlockSpec((hs[0].shape[0], tile), lambda i: (0, i))
    row = pl.BlockSpec((tile, D), lambda i: (i, 0))
    vec = pl.BlockSpec((1, D), lambda i: (0, 0))
    sds = jax.ShapeDtypeStruct
    return pl.pallas_call(
        functools.partial(mlp_out_kernel, nk, nc, nz),
        grid=(tok // tile,),
        in_specs=[pl.BlockSpec(memory_space=pltpu.SMEM)] + [wspec] * len(flat) + [hspec] * (3 * nk) + [row, vec, row],
        out_specs=[row, row, row, vec],
        out_shape=[sds((tok, D), BF16), sds((tok, D), F32), sds((tok, D), BF16), sds((1, D), F32)],
        scratch_shapes=[pltpu.VMEM((tile, D), F32)] * 2,
        compiler_params=pltpu.CompilerParams(vmem_limit_bytes=58 * MIB),
        cost_estimate=pl.CostEstimate(flops=18 * 10**9, bytes_accessed=45 * 10**6, transcendentals=0),
        name="mlp_out",
    )(zs, *flat, *hs, *dgs, *dus, h1, gain, dy)


def tokens_kernel(n, *refs):
    parts, (wq_ref, wk_ref, wv_ref, x_ref, gain_ref, dh1_ref, out_ref, dgain_ref) = refs[: 3 * n], refs[3 * n :]
    i = pl.program_id(0)
    total = None
    for j, w_ref in enumerate((wq_ref, wk_ref, wv_ref)):
        d = parts[j * n][...] if n == 1 else jnp.concatenate([r[...] for r in parts[j * n : (j + 1) * n]], axis=1)
        t = nt(d, w_ref[...])
        total = t if total is None else total + t
    dv, dgain = norm_back(x_ref[...].astype(F32), gain_ref[...], total)
    out_ref[...] = dh1_ref[...] + dv

    @pl.when(i == 0)
    def _():
        dgain_ref[...] = jnp.zeros_like(dgain_ref)

    dgain_ref[...] += dgain


def tokens_grad(dqs, dks, dvs, wq, wk, wv, x, gain, dh1):
    n = len(dqs)
    tok = x.shape[0]
    tile = 256
    row = pl.BlockSpec((tile, D), lambda i: (i, 0))
    full = pl.BlockSpec((D, D), lambda i: (0, 0))
    vec = pl.BlockSpec((1, D), lambda i: (0, 0))
    sds = jax.ShapeDtypeStruct
    return pl.pallas_call(
        functools.partial(tokens_kernel, n),
        grid=(tok // tile,),
        in_specs=[pl.BlockSpec((tile, d.shape[1]), lambda i: (i, 0)) for d in (*dqs, *dks, *dvs)] + [full, full, full, row, vec, row],
        out_specs=[row, vec],
        out_shape=[sds((tok, D), F32), sds((1, D), F32)],
        compiler_params=pltpu.CompilerParams(vmem_limit_bytes=40 * MIB),
        cost_estimate=pl.CostEstimate(flops=7 * 10**9, bytes_accessed=24 * 10**6, transcendentals=0),
        name="tokens_grad",
    )(*dqs, *dks, *dvs, wq, wk, wv, x, gain, dh1)
RING = (0, 1, 3, 2)


def ring_perm(step):
    n = len(RING)
    return [(RING[i], RING[(i + step) % n]) for i in range(n)]


def to_right(v):
    return lax.ppermute(v, "ha", ring_perm(1))


def to_left(v):
    return lax.ppermute(v, "ha", ring_perm(-1))


def along(v, step, n):
    return lax.ppermute(v, "ma", [(i, (i + step) % n) for i in range(n)])


def swap(v):
    return lax.ppermute(v, "rows", [(0, 1), (1, 0)])


def add(*vs):
    total = vs[0].astype(F32)
    for v in vs[1:]:
        total = total + v.astype(F32)
    return total.astype(BF16)


def gather_weights(own, nz):
    col = [own] + [along(own, s, nz) for s in range(1, nz)]
    left = [to_right(p) for p in col]
    right = [to_left(p) for p in col]
    cut = nz // 2
    far = [to_right(p) for p in left[:cut]] + [to_left(p) for p in right[cut:]]
    return [[b, [swap(p) for p in b]] for b in (col, left, far, right)]


def scatter_weights(grads, nz):
    cut = nz // 2
    mine = [g[0] for g in grads]
    got = [swap(g[1]) for g in grads]
    block = lambda k, s: (mine[k][s], got[k][s])
    far = [to_left(add(*block(2, s))) if s < cut else to_right(add(*block(2, s))) for s in range(nz)]
    from_right = [to_left(add(*block(1, s), *([far[s]] if s < cut else []))) for s in range(nz)]
    from_left = [to_right(add(*block(3, s), *([far[s]] if s >= cut else []))) for s in range(nz)]
    total = [add(*block(0, s), from_right[s], from_left[s]) for s in range(nz)]
    return add(total[0], *[along(total[s], -s, nz) for s in range(1, nz)])


def reduce_all(mine, other, nz):
    lead, width = mine.shape[:-2], mine.shape[-1]
    piece = mine.shape[-2] // (4 * nz)
    axis = len(lead)
    shape = (*lead, 4, nz, piece, width)
    mine, got = mine.reshape(shape), swap(other).reshape(shape)
    cut = nz // 2
    take = lambda v, k, lo, hi: lax.slice_in_dim(lax.index_in_dim(v, k, axis, keepdims=False), lo, hi, axis=axis)
    block = lambda k, lo=0, hi=nz: (take(mine, k, lo, hi), take(got, k, lo, hi))
    far_a = to_left(add(*block(2, 0, cut)))
    far_b = to_right(add(*block(2, cut, nz)))
    from_right = [to_left(add(*block(1, 0, cut), far_a)), to_left(add(*block(1, cut, nz)))]
    from_left = [to_right(add(*block(3, 0, cut))), to_right(add(*block(3, cut, nz), far_b))]
    total = [add(*block(0, 0, cut), from_right[0], from_left[0]), add(*block(0, cut, nz), from_right[1], from_left[1])]
    pick = lambda s: lax.index_in_dim(total[s // cut], s % cut, axis, keepdims=False)
    own = add(pick(0), *[along(pick(s), -s, nz) for s in range(1, nz)])
    col = [own] + [along(own, s, nz) for s in range(1, nz)]
    halves = jnp.stack(col[:cut]), jnp.stack(col[cut:])
    left = [to_right(v) for v in halves]
    right = [to_left(v) for v in halves]
    far = [to_right(left[0]), to_left(right[1])]
    blocks = jnp.stack([jnp.concatenate(b) for b in (halves, left, far, right)])
    return jnp.stack([blocks, swap(blocks)])


def place(order, sums):
    n = sums.shape[0] * sums.shape[1] * sums.shape[2]
    lead, piece, width = sums.shape[3:]
    flat = sums.reshape(n, lead, piece, width)

    def kernel(order_ref, in_ref, out_ref):
        for i in range(n):
            at = pl.ds(pl.multiple_of(order_ref[i] * piece, piece), piece)
            for j in range(lead):
                out_ref[j, at, :] = in_ref[i, j].astype(F32)

    vm = pl.BlockSpec(memory_space=pltpu.VMEM)
    return pl.pallas_call(
        kernel,
        in_specs=[pl.BlockSpec(memory_space=pltpu.SMEM), vm],
        out_specs=vm,
        out_shape=jax.ShapeDtypeStruct((lead, n * piece, width), F32),
        compiler_params=pltpu.CompilerParams(vmem_limit_bytes=30 * MIB),
        cost_estimate=pl.CostEstimate(flops=0, bytes_accessed=6 * flat.size, transcendentals=0),
        name="place",
    )(order, flat)


def body(
    paired, tokens, first_values, lengths, w_query, w_key, w_value, w_out, norm_attn, norm_mlp, w_gate, w_up, w_down, grad_out
):
    nz = lax.axis_size("ma")
    z = lax.axis_index("ma")
    r = lax.axis_index("rows")
    cos, sin = (jnp.asarray(t) for t in rope_tables())
    gain_a, gain_m = norm_attn[None], norm_mlp[None]
    tile = jnp.stack([w_gate.T, w_up.T, w_down])
    dz = tile.shape[2]
    if paired:
        fs = tile.shape[1] // 2
        own = lax.dynamic_slice_in_dim(tile, r * fs, fs, axis=1)
        blocks = gather_weights(own, nz)
        s = jnp.arange(nz, dtype=jnp.int32)
        zs = (z - s) % nz
        place_on_ring = jnp.asarray(np.argsort(RING), jnp.int32)[lax.axis_index("ha")]
        owners = jnp.asarray(RING, jnp.int32)[(place_on_ring - jnp.arange(4, dtype=jnp.int32)) % 4]
        halves = jnp.stack([r, 1 - r])
        order = ((halves[:, None, None] * 4 + owners[None, :, None]) * nz + zs[None, None, :]).reshape(-1)
        n = 8 * nz
    else:
        full = lax.all_gather(lax.all_gather(tile, "ma", axis=0), "ha", axis=0)
        blocks = [[[full[k, s] for s in range(nz)]] for k in range(lax.axis_size("ha"))]
        zs = jnp.arange(nz, dtype=jnp.int32)
        order, n = zs, 1
    q, k, v, o, st, nma, h1, nmm = attention_forward(
        lengths, tokens, gain_a, w_query, w_key, w_value, first_values, cos, sin, w_out, gain_m
    )
    nmat, ot, nmmt, dyt = prepare(order, n, nma, o, nmm, grad_out)
    turn_order = (0, 1, 3, 2)
    done = {i: mlp_block(zs, blocks[i], nmmt, dyt, nmm, grad_out) for i in turn_order}
    hs, dgs, dus = ([done[i][j] for i in range(4)] for j in range(3))
    mixed, dh1, da, dgain_m = mlp_out(zs, blocks, hs, dgs, dus, h1, gain_m, grad_out)
    wo_parts = wout_grad(ot, da)
    calls = [
        attention_backward(2 * i, 2, lengths, da, w_out, q, k, v, o, st, nmat, cos, sin) for i in range(2)
    ]
    dqs, dks, dvs, firsts, mines, others = zip(*calls)
    grad_tokens, dgain_a = tokens_grad(dqs, dks, dvs, w_query, w_key, w_value, tokens, gain_a, dh1)
    grad_first = jnp.concatenate(firsts, axis=1)
    if paired:
        tiles = scatter_weights([done[i][3:] for i in range(4)], nz)
        twin = swap(tiles)
        tiles = jnp.where(r == 0, jnp.concatenate([tiles, twin], axis=1), jnp.concatenate([twin, tiles], axis=1)).astype(F32)
        grad_wout = place(order, reduce_all(wo_parts[0][None], wo_parts[1][None], nz))[0]
        parts = [place(order, reduce_all(m, t, nz)) for m, t in zip(mines, others)]
        grad_q, grad_k, grad_v = (jnp.concatenate([p[j] for p in parts], axis=1) for j in range(3))
    else:
        stacked = jnp.stack([done[i][3] for i in range(4)])
        part = lax.psum_scatter(lax.psum_scatter(stacked, "ha", scatter_dimension=0), "ma", scatter_dimension=0)
        tiles = lax.psum(part, "rows").astype(F32)
        whole = [jnp.concatenate(wo_parts, axis=0)] + [
            jnp.concatenate([jnp.concatenate([m[j], t[j]], axis=0) for m, t in zip(mines, others)], axis=1) for j in range(3)
        ]
        grad_wout, grad_q, grad_k, grad_v = (g.astype(F32) for g in lax.psum(whole, ("rows", "ha", "ma")))
    gains = lax.psum((dgain_a, dgain_m), ("rows", "ha", "ma"))
    return (
        mixed, grad_tokens, grad_first, grad_q, grad_k, grad_v, grad_wout, gains[0][0], gains[1][0],
        tiles[0].T, tiles[1].T, tiles[2],
    )


def solution(mesh):
    tok = P(("rows", "ha", "ma"), None)
    gate, down = P("ma", "ha"), P("ha", "ma")
    return jax.shard_map(
        functools.partial(body, mesh.shape["rows"] == 2),
        mesh=mesh,
        in_specs=(tok, tok, P(("rows", "ha", "ma")), P(), P(), P(), P(), P(), P(), gate, gate, down, tok),
        out_specs=(tok, tok, tok, P(), P(), P(), P(), P(), P(), gate, gate, down),
        check_vma=False,
    )
```

time: 1230 us -> 643 us (0.52)
  waiting for transfers between devices: 705 us -> 176 us
  matrix products: 303 us -> 0 us
  Pallas kernels: 0 us -> 220 us
  starting transfers between devices: 0.48 us -> 118 us
  other arithmetic: 95.9 us -> 30.7 us
  local copies, waits for them, and re-layouts: 54.2 us -> 33.8 us
  between operations: 16.2 us -> 2.94 us
    dot_general x33 -> x0, matrix products: 303 us -> none  [the longest x14 116 us: contract(): lax.dot_general(left, right, (((left_dim,), (right_dim,)), ((), ())), pre...]
    reduce_scatter x5 -> x0, waiting for transfers between devices: 274 us -> none  [the longest x1 156 us: body(): lax.psum_scatter(contract(gate_rows, gate_all, 1, 1) + contract(upper_row...]
    all_gather x5 -> x0, waiting for transfers between devices: 224 us -> none  [the longest x1 88.5 us: body(): features = lax.all_gather(normed_m, 'ha', axis=0, tiled=True)]
    pallas_call x0 -> x14, Pallas kernels: none -> 220 us  [the longest x4 65.6 us: mlp_block(): pl.pallas_call(functools.partial(mlp_kernel, nc, nz), in_specs=[pl.BlockS...]
    psum x2 -> x0, waiting for transfers between devices: 205 us -> none  [the longest x1 205 us: body(): lax.psum((grad_wq, grad_wk, grad_wv, grad_wout, grad_gain_attn, grad_gain...]
    ppermute x0 -> x111, waiting for transfers between devices: none -> 176 us  [the longest x24 59 us: along(): return lax.ppermute(v, 'ma', [(i, (i + step) % n) for i in range(n)])]
    ppermute x0 -> x111, starting transfers between devices: none -> 118 us  [the longest x24 43 us: along(): return lax.ppermute(v, 'ma', [(i, (i + step) % n) for i in range(n)])]
    convert_element_type x6 -> x23, other arithmetic: 46.3 us -> 8.22 us  [the longest x22 8.01 us: add(): return total.astype(BF16)]
  transfers between devices with their start and end apart: 12 -> 111, of which waited for: 8 -> 43; matrix products, arithmetic and copies ran while one was open for 32% -> 5% of each run, Pallas kernels for 0% -> 26%
where the time goes in v1:
time: 643 us; the launch traced here: 635 us
  Pallas kernels  220 us (34%)
  waiting for transfers between devices  176 us (27%)
  starting transfers between devices  118 us (18%)
  blocking collectives  53.3 us (8%)
  local copies, waits for them, and re-layouts  33.8 us (5%)
  other arithmetic  30.7 us (5%)
    pallas_call x4, Pallas kernels, mlp_block(): pl.pallas_call(functools.partial(mlp_kernel, nc, nz), in_specs=[pl.BlockS...  65.6 us
    ppermute x24, waiting for transfers between devices, along(): return lax.ppermute(v, 'ma', [(i, (i + step) % n) for i in range(n)])  59 us
    ppermute x30, waiting for transfers between devices, to_left(): return lax.ppermute(v, 'ha', ring_perm(-1))  58.7 us
    ppermute x30, waiting for transfers between devices, to_right(): return lax.ppermute(v, 'ha', ring_perm(1))  56.3 us
    pallas_call x2, Pallas kernels, attention_backward(): pl.pallas_call(functools.partial(bwd_kernel, first_group), grid_spec=pltp...  53.7 us
    psum x1, blocking collectives, body(): gains = lax.psum((dgain_a, dgain_m), ('rows', 'ha', 'ma'))  53.3 us
    ppermute x24, starting transfers between devices, along(): return lax.ppermute(v, 'ma', [(i, (i + step) % n) for i in range(n)])  43 us
    pallas_call x1, Pallas kernels, attention_forward(): pl.pallas_call(fwd_kernel, grid_spec=pltpu.PrefetchScalarGridSpec(num_sca...  40.6 us
  transfers between devices with their start and end apart: 111, of which 43 were waited for; matrix products, arithmetic and copies ran while one was open for 5% of the time, Pallas kernels for 26%

profile of v1, /device:TPU:0, one launch (start us, length us, event | category | flops | bytes accessed | tf_op | source)
XLA Modules:
  0.0 634.8 jit_solution(16065776010555788310)
XLA Ops:
  10.8 9.3 %collective-permute-done.refs_1_ = bf16[3,352,256]{2,1,0:T(8,128)(2,1)S(1)} collective-permute-done((bf16[3,352,256]{2,1,0:T(8,128)(2,1)S(1)}, bf16[3,352,256]{2,1,0:T(8,128)(2,1)S(1)}, u32[]{:S(2)}, u32[]{:S(2)}) %collective-permute-start) | collective-permute-done | bytes 540704 | tf_op jit(solution)/shard_map/ppermute | solution.py:487
  20.2 22.4 %collective-permute-done.1.refs_2_ = bf16[3,352,256]{2,1,0:T(8,128)(2,1)} collective-permute-done((bf16[3,352,256]{2,1,0:T(8,128)(2,1)S(1)}, bf16[3,352,256]{2,1,0:T(8,128)(2,1)}, u32[]{:S(2)}, u32[]{:S(2)}) %collective-permute-start.1) | collective-permute-done | bytes 540704 | tf_op jit(solution)/shard_map/ppermute | solution.py:487
  49.7 8.1 %collective-permute-done.8.refs_1_.refs_9_ = bf16[3,352,256]{2,1,0:T(8,128)(2,1)S(1)} collective-permute-done((bf16[3,352,256]{2,1,0:T(8,128)(2,1)S(1)}, bf16[3,352,256]{2,1,0:T(8,128)(2,1)S(1)}, u32[]{:S(2)}, u32[]{:S(2)}) %collective-permute-start.8) | collective-permute-done | bytes 540704 | tf_op jit(solution)/shard_map/ppermute | solution.py:479
  58.5 40.6 %attention_forward.1 = (bf16[1024,1024]{1,0:T(8,128)(2,1)}, bf16[1024,1024]{1,0:T(8,128)(2,1)}, bf16[1024,1024]{1,0:T(8,128)(2,1)}, bf16[1024,1024]{1,0:T(8,128)...) custom-call(s32[1]{0:T(128)S(6)} %copy.109.len_ref, ...), custom_call_target="tpu_custom_call" | custom-call | flops 30000001024 | bytes 40000000 | tf_op jit(solution)/shard_map/attention_forward/pallas_call | solution.py:153
  110.0 3.2 prepare.1
  117.6 9.3 %collective-permute-done.10.refs_3_.refs_11_ = bf16[3,352,256]{2,1,0:T(8,128)(2,1)} collective-permute-done((bf16[3,352,256]{2,1,0:T(8,128)(2,1)}, bf16[3,352,256]{2,1,0:T(8,128)(2,1)}, u32[]{:S(2)}, u32[]{:S(2)}) %collective-permute-start.10) | collective-permute-done | bytes 540704 | tf_op jit(solution)/shard_map/ppermute | solution.py:479
  129.0 16.2 %mlp_block.4 = (bf16[704,1024]{1,0:T(8,128)(2,1)S(1)}, bf16[704,1024]{1,0:T(8,128)(2,1)S(1)}, bf16[704,1024]{1,0:T(8,128)(2,1)S(1)}, bf16[4,3,352,256]{3,2,1,0:T(8,128)(2,1)}, bf16[4,3,352,256]{3,2,1,0:T(8,128)(2,1)}) custom-call(s32[4]{0:T(128)S(1)} %and_select_fusion.1.zs_ref, bf16[3,352,256]{2,1,0:T(8,128)(2,1)S(1)} %fusion.22.refs_0_, ...), custom_call_target="tpu_custom_call" | custom-call | flops 8858370048 | bytes 15000000 | tf_op jit(solution)/shard_map/mlp_block/pallas_call | solution.py:357
  151.7 16.3 %mlp_block.7 = (bf16[704,1024]{1,0:T(8,128)(2,1)S(1)}, bf16[704,1024]{1,0:T(8,128)(2,1)S(1)}, bf16[704,1024]{1,0:T(8,128)(2,1)S(1)}, bf16[4,3,352,256]{3,2,1,0:T(8,128)(2,1)}, bf16[4,3,352,256]{3,2,1,0:T(8,128)(2,1)}) custom-call(s32[4]{0:T(128)S(1)} %and_select_fusion.1.zs_ref, bf16[3,352,256]{2,1,0:T(8,128)(2,1)} %collective-permute-done.25.refs_0_.refs_24_, ...), custom_call_target="tpu_custom_call" | custom-call | flops 8858370048 | bytes 15000000 | tf_op jit(solution)/shard_map/mlp_block/pallas_call | solution.py:357
  171.8 3.3 collective-permute-done.20.refs_3_.refs_19_
  175.7 16.5 %mlp_block.5 = (bf16[704,1024]{1,0:T(8,128)(2,1)S(1)}, bf16[704,1024]{1,0:T(8,128)(2,1)S(1)}, bf16[704,1024]{1,0:T(8,128)(2,1)S(1)}, bf16[4,3,352,256]{3,2,1,0:T(8,128)(2,1)}, bf16[4,3,352,256]{3,2,1,0:T(8,128)(2,1)}) custom-call(s32[4]{0:T(128)S(1)} %and_select_fusion.1.zs_ref, bf16[3,352,256]{2,1,0:T(8,128)(2,1)} %collective-permute-done.7.refs_0_.refs_8_, ...), custom_call_target="tpu_custom_call" | custom-call | flops 8858370048 | bytes 15000000 | tf_op jit(solution)/shard_map/mlp_block/pallas_call | solution.py:357
  195.6 16.6 %mlp_block.6 = (bf16[704,1024]{1,0:T(8,128)(2,1)S(1)}, bf16[704,1024]{1,0:T(8,128)(2,1)S(1)}, bf16[704,1024]{1,0:T(8,128)(2,1)S(1)}, bf16[4,3,352,256]{3,2,1,0:T(8,128)(2,1)}, bf16[4,3,352,256]{3,2,1,0:T(8,128)(2,1)}) custom-call(s32[4]{0:T(128)S(1)} %and_select_fusion.1.zs_ref, bf16[3,352,256]{2,1,0:T(8,128)(2,1)} %collective-permute-done.15.refs_0_.refs_16_, ...), custom_call_target="tpu_custom_call" | custom-call | flops 8858370048 | bytes 15000000 | tf_op jit(solution)/shard_map/mlp_block/pallas_call | solution.py:357
  215.6 38.6 %mlp_out.1 = (bf16[1024,1024]{1,0:T(8,128)(2,1)}, f32[1024,1024]{1,0:T(8,128)}, bf16[1024,1024]{1,0:T(8,128)(2,1)}, f32[1,1024]{1,0:T(1,128)}) custom-call(s32[4]{0:T(128)} %copy-done.5, bf16[3,352,256]{2,1,0:T(8,128)(2,1)} %copy-done.4, bf16[3,352,256]{2,1,0:T(8,128)(2,1)} %copy-done.12, bf16[3,352,256]{2,1,0:T(8,128)(2,1)} %collective-permute-done.1.refs_2_, ...), custom_call_target="tpu_custom_call" | custom-call | flops 17999998976 | bytes 45000000 | tf_op jit(solution)/shard_map/mlp_out/pallas_call | solution.py:421
  263.4 26.9 %attention_backward.2 = (bf16[1024,512]{1,0:T(8,128)(2,1)}, bf16[1024,512]{1,0:T(8,128)(2,1)}, bf16[1024,512]{1,0:T(8,128)(2,1)}, f32[1024,512]{1,0:T(8,128)}, b...) custom-call(s32[1]{0:T(128)S(6)} %copy.109.len_ref, bf16[1024,1024]{1,0:T(8,128)(2,1)} %get-tuple-element.83.da_ref, ...), custom_call_target="tpu_custom_call" | custom-call | flops 20000000000 | bytes 10000000 | tf_op jit(solution)/shard_map/attention_backward/pallas_call | solution.py:301
  299.1 26.8 %attention_backward.3 = (bf16[1024,512]{1,0:T(8,128)(2,1)}, bf16[1024,512]{1,0:T(8,128)(2,1)}, bf16[1024,512]{1,0:T(8,128)(2,1)}, f32[1024,512]{1,0:T(8,128)}, b...) custom-call(s32[1]{0:T(128)S(6)} %copy.109.len_ref, bf16[1024,1024]{1,0:T(8,128)(2,1)} %get-tuple-element.83.da_ref, ...), custom_call_target="tpu_custom_call" | custom-call | flops 20000000000 | bytes 10000000 | tf_op jit(solution)/shard_map/attention_backward/pallas_call | solution.py:301
  328.2 12.4 %collective-permute-start.80 = (bf16[1,32,1024]{2,1,0:T(8,128)(2,1)S(1)}, bf16[1,32,1024]{2,1,0:T(8,128)(2,1)S(1)}, u32[]{:S(2)}, u32[]{:S(2)}) collective-permute-start(bf16[1,32,1024]{2,1,0:T(8,128)(2,1)S(1)} %get-tuple-element.203), channel_id=1, source_target_pairs={{0,1},{1,2},{2,3},{3,0},{4,5},{5,6},{6,7},{7,4},{8,9},{9,10},{10,1... | collective-permute-start | bytes 196616 | tf_op jit(solution)/shard_map/ppermute | solution.py:487
  340.9 3.4 collective-permute-done.80
  348.4 3.4 collective-permute-done.82
  353.5 4.4 collective-permute-done.81
  370.5 3.8 collective-permute-done.86
  392.3 3.5 collective-permute-done.53
  403.8 4.6 collective-permute-done.39
  412.3 5.8 collective-permute-done.59
  418.1 3.8 collective-permute-start.42
  446.0 17.6 %collective-permute-done.64 = bf16[2,3,32,512]{3,2,1,0:T(8,128)(2,1)S(1)} collective-permute-done((bf16[2,3,32,512]{3,2,1,0:T(8,128)(2,1)S(1)}, bf16[2,3,32,512]{3,2,1,0:T(8,128)(2,1)S(1)}, u32[]{:S(2)}, u32[]{:S(2)}) %collective-permute-start.64) | collective-permute-done | bytes 196640 | tf_op jit(solution)/shard_map/ppermute | solution.py:479
  477.2 6.7 %collective-permute-done.102 = bf16[3,352,256]{2,1,0:T(8,128)(2,1)S(1)} collective-permute-done((bf16[3,352,256]{2,1,0:T(8,128)(2,1)S(1)}, bf16[3,352,256]{2,1,0:T(8,128)(2,1)S(1)}, u32[]{:S(2)}, u32[]{:S(2)}) %collective-permute-start.102) | collective-permute-done | bytes 540704 | tf_op jit(solution)/shard_map/ppermute | solution.py:483
  485.0 10.4 %collective-permute-done.106 = bf16[3,352,256]{2,1,0:T(8,128)(2,1)S(1)} collective-permute-done((bf16[3,352,256]{2,1,0:T(8,128)(2,1)S(1)}, bf16[3,352,256]{2,1,0:T(8,128)(2,1)S(1)}, u32[]{:S(2)}, u32[]{:S(2)}) %collective-permute-start.106) | collective-permute-done | bytes 540704 | tf_op jit(solution)/shard_map/ppermute | solution.py:483
  496.7 10.4 %collective-permute-done.94 = bf16[3,352,256]{2,1,0:T(8,128)(2,1)S(1)} collective-permute-done((bf16[3,352,256]{2,1,0:T(8,128)(2,1)S(1)}, bf16[3,352,256]{2,1,0:T(8,128)(2,1)S(1)}, u32[]{:S(2)}, u32[]{:S(2)}) %collective-permute-start.94) | collective-permute-done | bytes 540704 | tf_op jit(solution)/shard_map/ppermute | solution.py:483
  507.0 11.6 %collective-permute-done.98 = bf16[3,352,256]{2,1,0:T(8,128)(2,1)S(1)} collective-permute-done((bf16[3,352,256]{2,1,0:T(8,128)(2,1)S(1)}, bf16[3,352,256]{2,1,0:T(8,128)(2,1)S(1)}, u32[]{:S(2)}, u32[]{:S(2)}) %collective-permute-start.98) | collective-permute-done | bytes 540704 | tf_op jit(solution)/shard_map/ppermute | solution.py:483
  536.2 3.4 collective-permute-done.97
  543.7 11.1 %tokens_grad.1 = (f32[1024,1024]{1,0:T(8,128)}, f32[1,1024]{1,0:T(1,128)S(1)}) custom-call(bf16[1024,512]{1,0:T(8,128)(2,1)S(1)} %copy-done.33, bf16[1024,512]{1,0:T(8,128)(2,1)S(1)} %copy-done.36, bf16[1024,512]{1,0:T(8,128)(2,1)S(1)} %copy-done.34, bf16[1024,512]{1,0:T(8,128)(2,1)S(1)} %copy-done.37, bf16[1024,512]{1,0:T(8,128)(2,1)S(1)} %copy-done.35, ...), custom_call_target="tpu_custom_call" | custom-call | flops 7000000000 | bytes 24000000 | tf_op jit(solution)/shard_map/tokens_grad/pallas_call | solution.py:460
  554.8 53.3 %all-reduce = (f32[1024]{0:T(1024)}, f32[1024]{0:T(1024)}) all-reduce(f32[1024]{0:T(1024)S(1)} %bitcast.252, f32[1024]{0:T(1024)S(1)} %bitcast.290), channel_id=1, replica_groups=mesh['rows'=2,'ha'=4,'ma'=4] {'rows','ha','ma'}, use_global_device_ids=true, to_apply=%region_0.1 | all-reduce | flops 2048 | bytes 16384 | tf_op jit(solution)/shard_map/psum | solution.py:626
  608.1 4.9 pad_maximum_fusion
  (429 shorter events, 203.2 us)
Async XLA Ops:
  4.9 37.7 %collective-permute-start.1 = (bf16[3,352,256]{2,1,0:T(8,128)(2,1)S(1)}, bf16[3,352,256]{2,1,0:T(8,128)(2,1)}, u32[]{:S(2)}, u32[]{:S(2)}) collective-permute-start(bf16[3,352,256]{2,1,0:T(8,128)(2,1)S(1)} %fusion.22.refs_0_), channel_id=1, source_target_pairs={{0,2},{1,3},{2,0},{3,1},{4,6},{5,7},{6,4},{7,5},{8,10},{9,11},{10,... | collective-permute-start | bytes 1622024 | tf_op jit(solution)/shard_map/ppermute | solution.py:487
  7.5 37.3 %collective-permute-start.2 = (bf16[3,352,256]{2,1,0:T(8,128)(2,1)S(1)}, bf16[3,352,256]{2,1,0:T(8,128)(2,1)}, u32[]{:S(2)}, u32[]{:S(2)}) collective-permute-start(bf16[3,352,256]{2,1,0:T(8,128)(2,1)S(1)} %fusion.22.refs_0_), channel_id=1, source_target_pairs={{0,3},{1,0},{2,1},{3,2},{4,7},{5,4},{6,5},{7,6},{8,11},{9,8},{10,9... | collective-permute-start | bytes 1622024 | tf_op jit(solution)/shard_map/ppermute | solution.py:487
  8.8 36.5 %collective-permute-start.7 = (bf16[3,352,256]{2,1,0:T(8,128)(2,1)S(1)}, bf16[3,352,256]{2,1,0:T(8,128)(2,1)}, u32[]{:S(2)}, u32[]{:S(2)}) collective-permute-start(bf16[3,352,256]{2,1,0:T(8,128)(2,1)S(1)} %fusion.22.refs_0_), channel_id=1, source_target_pairs={{0,4},{4,12},{12,8},{8,0},{1,5},{5,13},{13,9},{9,1},{2,6},{6,14},{... | collective-permute-start | bytes 1622024 | tf_op jit(solution)/shard_map/ppermute | solution.py:479
  10.3 36.6 %collective-permute-start.25 = (bf16[3,352,256]{2,1,0:T(8,128)(2,1)S(1)}, bf16[3,352,256]{2,1,0:T(8,128)(2,1)}, u32[]{:S(2)}, u32[]{:S(2)}) collective-permute-start(bf16[3,352,256]{2,1,0:T(8,128)(2,1)S(1)} %fusion.22.refs_0_), channel_id=1, source_target_pairs={{0,8},{4,0},{12,4},{8,12},{1,9},{5,1},{13,5},{9,13},{2,10},{6,2},{... | collective-permute-start | bytes 1622024 | tf_op jit(solution)/shard_map/ppermute | solution.py:483
  20.2 28.2 %collective-permute-start.3 = (bf16[3,352,256]{2,1,0:T(8,128)(2,1)S(1)}, bf16[3,352,256]{2,1,0:T(8,128)(2,1)S(1)}, u32[]{:S(2)}, u32[]{:S(2)}) collective-permute-start(bf16[3,352,256]{2,1,0:T(8,128)(2,1)S(1)} %fusion.22.refs_0_), channel_id=1, source_target_pairs={{0,16},{16,0},{1,17},{17,1},{2,18},{18,2},{3,19},{19,3},{4,20},{20... | collective-permute-start | bytes 1622024 | tf_op jit(solution)/shard_map/ppermute | solution.py:491
  44.7 59.6 %collective-permute-start.26 = (bf16[3,352,256]{2,1,0:T(8,128)(2,1)S(1)}, bf16[3,352,256]{2,1,0:T(8,128)(2,1)}, u32[]{:S(2)}, u32[]{:S(2)}) collective-permute-start(bf16[3,352,256]{2,1,0:T(8,128)(2,1)S(1)} %collective-permute-done.refs_1_), channel_id=1, source_target_pairs={{0,8},{4,0},{12,4},{8,12},{1,9},{5,1},{13,5},{9,13},{2,10},{6,2},{... | collective-permute-start | bytes 1622024 | tf_op jit(solution)/shard_map/ppermute | solution.py:483
  45.3 55.8 %collective-permute-start.17 = (bf16[3,352,256]{2,1,0:T(8,128)(2,1)}, bf16[3,352,256]{2,1,0:T(8,128)(2,1)}, u32[]{:S(2)}, u32[]{:S(2)}) collective-permute-start(bf16[3,352,256]{2,1,0:T(8,128)(2,1)} %collective-permute-done.1.refs_2_), channel_id=1, source_target_pairs={{0,8},{4,0},{12,4},{8,12},{1,9},{5,1},{13,5},{9,13},{2,10},{6,2},{... | collective-permute-start | bytes 1622024 | tf_op jit(solution)/shard_map/ppermute | solution.py:483
  46.9 55.8 %collective-permute-start.19 = (bf16[3,352,256]{2,1,0:T(8,128)(2,1)}, bf16[3,352,256]{2,1,0:T(8,128)(2,1)}, u32[]{:S(2)}, u32[]{:S(2)}) collective-permute-start(bf16[3,352,256]{2,1,0:T(8,128)(2,1)} %collective-permute-done.2.refs_3_), channel_id=1, source_target_pairs={{0,8},{4,0},{12,4},{8,12},{1,9},{5,1},{13,5},{9,13},{2,10},{6,2},{... | collective-permute-start | bytes 1622024 | tf_op jit(solution)/shard_map/ppermute | solution.py:483
  49.2 55.2 %collective-permute-start.15 = (bf16[3,352,256]{2,1,0:T(8,128)(2,1)}, bf16[3,352,256]{2,1,0:T(8,128)(2,1)}, u32[]{:S(2)}, u32[]{:S(2)}) collective-permute-start(bf16[3,352,256]{2,1,0:T(8,128)(2,1)} %collective-permute-done.7.refs_0_.refs_8_), channel_id=1, source_target_pairs={{0,4},{4,12},{12,8},{8,0},{1,5},{5,13},{13,9},{9,1},{2,6},{6,14},{... | collective-permute-start | bytes 1622024 | tf_op jit(solution)/shard_map/ppermute | solution.py:479
  57.7 47.1 %collective-permute-start.27 = (bf16[3,352,256]{2,1,0:T(8,128)(2,1)}, bf16[3,352,256]{2,1,0:T(8,128)(2,1)}, u32[]{:S(2)}, u32[]{:S(2)}) collective-permute-start(bf16[3,352,256]{2,1,0:T(8,128)(2,1)} %collective-permute-done.25.refs_0_.refs_24_), channel_id=1, source_target_pairs={{0,16},{16,0},{1,17},{17,1},{2,18},{18,2},{3,19},{19,3},{4,20},{20... | collective-permute-start | bytes 1622024 | tf_op jit(solution)/shard_map/ppermute | solution.py:491
  117.2 31.5 %collective-permute-start.11 = (bf16[3,352,256]{2,1,0:T(8,128)(2,1)}, bf16[3,352,256]{2,1,0:T(8,128)(2,1)S(1)}, u32[]{:S(2)}, u32[]{:S(2)}) collective-permute-start(bf16[3,352,256]{2,1,0:T(8,128)(2,1)} %collective-permute-done.7.refs_0_.refs_8_), channel_id=1, source_target_pairs={{0,16},{16,0},{1,17},{17,1},{2,18},{18,2},{3,19},{19,3},{4,20},{20... | collective-permute-start | bytes 1622024 | tf_op jit(solution)/shard_map/ppermute | solution.py:491
  262.4 29.4 %collective-permute-start.72 = (bf16[1,2,32,1024]{3,2,1,0:T(8,128)(2,1)S(1)}, bf16[1,2,32,1024]{3,2,1,0:T(8,128)(2,1)S(1)}, u32[]{:S(2)}, u32[]{:S(2)}) collective-permute-start(bf16[1,2,32,1024]{3,2,1,0:T(8,128)(2,1)S(1)} %get-tuple-element.192), channel_id=1, source_target_pairs={{0,8},{4,0},{12,4},{8,12},{1,9},{5,1},{13,5},{9,13},{2,10},{6,2},{... | collective-permute-start | bytes 393224 | tf_op jit(solution)/shard_map/ppermute | solution.py:483
  291.9 34.1 %collective-permute-start.73 = (bf16[1,2,32,1024]{3,2,1,0:T(8,128)(2,1)S(1)}, bf16[1,2,32,1024]{3,2,1,0:T(8,128)(2,1)S(1)}, u32[]{:S(2)}, u32[]{:S(2)}) collective-permute-start(bf16[1,2,32,1024]{3,2,1,0:T(8,128)(2,1)S(1)} %get-tuple-element.190), channel_id=1, source_target_pairs={{0,8},{4,0},{12,4},{8,12},{1,9},{5,1},{13,5},{9,13},{2,10},{6,2},{... | collective-permute-start | bytes 393224 | tf_op jit(solution)/shard_map/ppermute | solution.py:483
  292.5 34.0 %collective-permute-start.76 = (bf16[1,2,32,1024]{3,2,1,0:T(8,128)(2,1)S(1)}, bf16[1,2,32,1024]{3,2,1,0:T(8,128)(2,1)S(1)}, u32[]{:S(2)}, u32[]{:S(2)}) collective-permute-start(bf16[1,2,32,1024]{3,2,1,0:T(8,128)(2,1)S(1)} %get-tuple-element.191), channel_id=1, source_target_pairs={{0,8},{4,0},{12,4},{8,12},{1,9},{5,1},{13,5},{9,13},{2,10},{6,2},{... | collective-permute-start | bytes 393224 | tf_op jit(solution)/shard_map/ppermute | solution.py:483
  295.8 30.6 %collective-permute-start.74 = (bf16[1,2,32,1024]{3,2,1,0:T(8,128)(2,1)S(1)}, bf16[1,2,32,1024]{3,2,1,0:T(8,128)(2,1)S(1)}, u32[]{:S(2)}, u32[]{:S(2)}) collective-permute-start(bf16[1,2,32,1024]{3,2,1,0:T(8,128)(2,1)S(1)} %get-tuple-element.194), channel_id=1, source_target_pairs={{0,4},{4,12},{12,8},{8,0},{1,5},{5,13},{13,9},{9,1},{2,6},{6,14},{... | collective-permute-start | bytes 393224 | tf_op jit(solution)/shard_map/ppermute | solution.py:479
  297.4 29.1 %collective-permute-start.78 = (bf16[1,2,32,1024]{3,2,1,0:T(8,128)(2,1)S(1)}, bf16[1,2,32,1024]{3,2,1,0:T(8,128)(2,1)S(1)}, u32[]{:S(2)}, u32[]{:S(2)}) collective-permute-start(bf16[1,2,32,1024]{3,2,1,0:T(8,128)(2,1)S(1)} %get-tuple-element.195), channel_id=1, source_target_pairs={{0,4},{4,12},{12,8},{8,0},{1,5},{5,13},{13,9},{9,1},{2,6},{6,14},{... | collective-permute-start | bytes 393224 | tf_op jit(solution)/shard_map/ppermute | solution.py:479
  325.9 32.8 %collective-permute-start.31 = (bf16[3,512,512]{2,1,0:T(8,128)(2,1)S(1)}, bf16[3,512,512]{2,1,0:T(8,128)(2,1)S(1)}, u32[]{:S(2)}, u32[]{:S(2)}) collective-permute-start(bf16[3,512,512]{2,1,0:T(8,128)(2,1)S(1)} %copy-done.69), channel_id=1, source_target_pairs={{0,16},{16,0},{1,17},{17,1},{2,18},{18,2},{3,19},{19,3},{4,20},{20... | collective-permute-start | bytes 4718600 | tf_op jit(solution)/shard_map/ppermute | solution.py:491
  326.0 34.5 %collective-permute-start.51 = (bf16[3,512,512]{2,1,0:T(8,128)(2,1)}, bf16[3,512,512]{2,1,0:T(8,128)(2,1)S(1)}, u32[]{:S(2)}, u32[]{:S(2)}) collective-permute-start(bf16[3,512,512]{2,1,0:T(8,128)(2,1)} %get-tuple-element.102), channel_id=1, source_target_pairs={{0,16},{16,0},{1,17},{17,1},{2,18},{18,2},{3,19},{19,3},{4,20},{20... | collective-permute-start | bytes 4718600 | tf_op jit(solution)/shard_map/ppermute | solution.py:491
  363.8 58.6 %collective-permute-start.93 = (bf16[4,3,352,256]{3,2,1,0:T(8,128)(2,1)S(1)}, bf16[4,3,352,256]{3,2,1,0:T(8,128)(2,1)S(1)}, u32[]{:S(2)}, u32[]{:S(2)}) collective-permute-start(bf16[4,3,352,256]{3,2,1,0:T(8,128)(2,1)S(1)} %copy-done.67), channel_id=1, source_target_pairs={{0,16},{16,0},{1,17},{17,1},{2,18},{18,2},{3,19},{19,3},{4,20},{20... | collective-permute-start | bytes 6488072 | tf_op jit(solution)/shard_map/ppermute | solution.py:491
  385.8 45.9 %collective-permute-start.91 = (bf16[4,3,352,256]{3,2,1,0:T(8,128)(2,1)S(1)}, bf16[4,3,352,256]{3,2,1,0:T(8,128)(2,1)S(1)}, u32[]{:S(2)}, u32[]{:S(2)}) collective-permute-start(bf16[4,3,352,256]{3,2,1,0:T(8,128)(2,1)S(1)} %copy-done.66), channel_id=1, source_target_pairs={{0,16},{16,0},{1,17},{17,1},{2,18},{18,2},{3,19},{19,3},{4,20},{20... | collective-permute-start | bytes 6488072 | tf_op jit(solution)/shard_map/ppermute | solution.py:491
  431.7 41.2 %collective-permute-start.103 = (bf16[3,352,256]{2,1,0:T(8,128)(2,1)S(1)}, bf16[3,352,256]{2,1,0:T(8,128)(2,1)S(1)}, u32[]{:S(2)}, u32[]{:S(2)}) collective-permute-start(bf16[3,352,256]{2,1,0:T(8,128)(2,1)S(1)} %get-tuple-element.128), channel_id=1, source_target_pairs={{0,4},{4,12},{12,8},{8,0},{1,5},{5,13},{13,9},{9,1},{2,6},{6,14},{... | collective-permute-start | bytes 1622024 | tf_op jit(solution)/shard_map/ppermute | solution.py:479
  433.8 39.7 %collective-permute-start.107 = (bf16[3,352,256]{2,1,0:T(8,128)(2,1)S(1)}, bf16[3,352,256]{2,1,0:T(8,128)(2,1)S(1)}, u32[]{:S(2)}, u32[]{:S(2)}) collective-permute-start(bf16[3,352,256]{2,1,0:T(8,128)(2,1)S(1)} %get-tuple-element.127), channel_id=1, source_target_pairs={{0,4},{4,12},{12,8},{8,0},{1,5},{5,13},{13,9},{9,1},{2,6},{6,14},{... | collective-permute-start | bytes 1622024 | tf_op jit(solution)/shard_map/ppermute | solution.py:479
  473.0 34.1 %collective-permute-start.94 = (bf16[3,352,256]{2,1,0:T(8,128)(2,1)S(1)}, bf16[3,352,256]{2,1,0:T(8,128)(2,1)S(1)}, u32[]{:S(2)}, u32[]{:S(2)}) collective-permute-start(bf16[3,352,256]{2,1,0:T(8,128)(2,1)S(1)} %get-tuple-element.126), channel_id=1, source_target_pairs={{0,8},{4,0},{12,4},{8,12},{1,9},{5,1},{13,5},{9,13},{2,10},{6,2},{... | collective-permute-start | bytes 1622024 | tf_op jit(solution)/shard_map/ppermute | solution.py:483
  473.4 45.2 %collective-permute-start.98 = (bf16[3,352,256]{2,1,0:T(8,128)(2,1)S(1)}, bf16[3,352,256]{2,1,0:T(8,128)(2,1)S(1)}, u32[]{:S(2)}, u32[]{:S(2)}) collective-permute-start(bf16[3,352,256]{2,1,0:T(8,128)(2,1)S(1)} %get-tuple-element.129), channel_id=1, source_target_pairs={{0,8},{4,0},{12,4},{8,12},{1,9},{5,1},{13,5},{9,13},{2,10},{6,2},{... | collective-permute-start | bytes 1622024 | tf_op jit(solution)/shard_map/ppermute | solution.py:483
  477.2 65.2 %collective-permute-start.90 = (bf16[4,4,1,32,1024]{4,3,1,0,2:T(8,128)(2,1)S(1)}, bf16[4,4,1,32,1024]{4,3,1,0,2:T(8,128)(2,1)S(1)}, u32[]{:S(2)}, u32[]{:S(2)}) collective-permute-start(bf16[4,4,1,32,1024]{4,3,1,0,2:T(8,128)(2,1)S(1)} %get-tuple-element.163), channel_id=1, source_target_pairs={{0,16},{16,0},{1,17},{17,1},{2,18},{18,2},{3,19},{19,3},{4,20},{20... | collective-permute-start | bytes 3145736 | tf_op jit(solution)/shard_map/ppermute | solution.py:491
  483.9 35.2 %collective-permute-start.46 = (bf16[2,3,32,512]{3,2,1,0:T(8,128)(2,1)S(1)}, bf16[2,3,32,512]{3,2,1,0:T(8,128)(2,1)S(1)}, u32[]{:S(2)}, u32[]{:S(2)}) collective-permute-start(bf16[2,3,32,512]{3,2,1,0:T(8,128)(2,1)S(1)} %collective-permute-done.44), channel_id=1, source_target_pairs={{0,4},{4,12},{12,8},{8,0},{1,5},{5,13},{13,9},{9,1},{2,6},{6,14},{... | collective-permute-start | bytes 589832 | tf_op jit(solution)/shard_map/ppermute | solution.py:479
  495.5 27.4 %collective-permute-start.48 = (bf16[2,3,32,512]{3,2,1,0:T(8,128)(2,1)S(1)}, bf16[2,3,32,512]{3,2,1,0:T(8,128)(2,1)S(1)}, u32[]{:S(2)}, u32[]{:S(2)}) collective-permute-start(bf16[2,3,32,512]{3,2,1,0:T(8,128)(2,1)S(1)} %collective-permute-done.47), channel_id=1, source_target_pairs={{0,8},{4,0},{12,4},{8,12},{1,9},{5,1},{13,5},{9,13},{2,10},{6,2},{... | collective-permute-start | bytes 589832 | tf_op jit(solution)/shard_map/ppermute | solution.py:483
  533.8 84.5 %collective-permute-start.50 = (bf16[4,4,3,32,512]{4,3,2,1,0:T(8,128)(2,1)}, bf16[4,4,3,32,512]{4,3,2,1,0:T(8,128)(2,1)}, u32[]{:S(2)}, u32[]{:S(2)}) collective-permute-start(bf16[4,4,3,32,512]{4,3,2,1,0:T(8,128)(2,1)} %get-tuple-element.143), channel_id=1, source_target_pairs={{0,16},{16,0},{1,17},{17,1},{2,18},{18,2},{3,19},{19,3},{4,20},{20... | collective-permute-start | bytes 4718600 | tf_op jit(solution)/shard_map/ppermute | solution.py:491
  533.9 87.8 %collective-permute-start.70 = (bf16[4,4,3,32,512]{4,3,2,1,0:T(8,128)(2,1)}, bf16[4,4,3,32,512]{4,3,2,1,0:T(8,128)(2,1)}, u32[]{:S(2)}, u32[]{:S(2)}) collective-permute-start(bf16[4,4,3,32,512]{4,3,2,1,0:T(8,128)(2,1)} %get-tuple-element.153), channel_id=1, source_target_pairs={{0,16},{16,0},{1,17},{17,1},{2,18},{18,2},{3,19},{19,3},{4,20},{20... | collective-permute-start | bytes 4718600 | tf_op jit(solution)/shard_map/ppermute | solution.py:491
  539.6 76.4 %collective-permute-start.101 = (bf16[3,352,256]{2,1,0:T(8,128)(2,1)}, bf16[3,352,256]{2,1,0:T(8,128)(2,1)}, u32[]{:S(2)}, u32[]{:S(2)}) collective-permute-start(bf16[3,352,256]{2,1,0:T(8,128)(2,1)} %get-tuple-element.132), channel_id=1, source_target_pairs={{0,3},{1,0},{2,1},{3,2},{4,7},{5,4},{6,5},{7,6},{8,11},{9,8},{10,9... | collective-permute-start | bytes 1622024 | tf_op jit(solution)/shard_map/ppermute | solution.py:487
  542.4 73.6 %collective-permute-start.105 = (bf16[3,352,256]{2,1,0:T(8,128)(2,1)}, bf16[3,352,256]{2,1,0:T(8,128)(2,1)}, u32[]{:S(2)}, u32[]{:S(2)}) collective-permute-start(bf16[3,352,256]{2,1,0:T(8,128)(2,1)} %get-tuple-element.134), channel_id=1, source_target_pairs={{0,2},{1,3},{2,0},{3,1},{4,6},{5,7},{6,4},{7,5},{8,10},{9,11},{10,... | collective-permute-start | bytes 1622024 | tf_op jit(solution)/shard_map/ppermute | solution.py:487
  542.5 73.6 %collective-permute-start.109 = (bf16[3,352,256]{2,1,0:T(8,128)(2,1)}, bf16[3,352,256]{2,1,0:T(8,128)(2,1)}, u32[]{:S(2)}, u32[]{:S(2)}) collective-permute-start(bf16[3,352,256]{2,1,0:T(8,128)(2,1)} %get-tuple-element.133), channel_id=1, source_target_pairs={{0,1},{1,2},{2,3},{3,0},{4,5},{5,6},{6,7},{7,4},{8,9},{9,10},{10,1... | collective-permute-start | bytes 1622024 | tf_op jit(solution)/shard_map/ppermute | solution.py:487
  (149 other events, 2153.2 us)
